TPU v7x, 32 devices: a whole 2x2x4 slice. The times are simulated.
32 devices in a mesh: req: 8 (over z, y), tp: 4 (over x, core).
Axes of the slice: x: 2, y: 2, z: 4, core: 2. Of those that a mesh axis runs over, the one named last changes fastest.
Arguments:
- states: bfloat16 [16, 512, 1024], P('req', 'tp'), may hold values from -45 to 45
- lengths: int32 [16], P('req'), may hold values from 3 to 512, as said below
- w_qkv: bfloat16 [1024, 3, 1024], P(None, None, 'tp'), may hold values from -0.1875 to 0.1875
- b_qkv: float32 [3, 1024], P(None, 'tp'), may hold values from -3 to 3
- w_out: bfloat16 [1024, 1024], P('tp'), may hold values from -0.1875 to 0.1875
- b_out: float32 [1024], replicated, may hold values from -3 to 3
- ln1_gain: float32 [1024], replicated, may hold values from 0.1 to 1.9
- ln1_shift: float32 [1024], replicated, may hold values from -3 to 3
- w_up: bfloat16 [1024, 4096], P(None, 'tp'), may hold values from -0.1875 to 0.1875
- b_up: float32 [4096], P('tp'), may hold values from -3 to 3
- w_down: bfloat16 [4096, 1024], P('tp'), may hold values from -0.09375 to 0.09375
- b_down: float32 [1024], replicated, may hold values from -3 to 3
- ln2_gain: float32 [1024], replicated, may hold values from 0.1 to 1.9
- ln2_shift: float32 [1024], replicated, may hold values from -3 to 3
- index_rows: bfloat16 [131072, 1024], P(('req', 'tp')), may hold values from -0.1875 to 0.1875
- cand_ids: int32 [16, 64], P('req', 'tp'), may hold values from 0 to 131071
Outputs:
- hidden_out: bfloat16 [16, 512, 1024], P('req', 'tp')
- scores: float32 [16, 64], P('req', 'tp')
Inputs may be any that keep to these rules, and one draw needn't show every extreme that they name: Valid positions are the first lengths ones of a text; in every draw some text has 512.
All inputs are finite; a program needn't handle non-finite values.
Results may differ from a plain program's by a relative error of at most 0.015.
Values may be sent and summed in bfloat16 or wider, within the bound.
No kernel may reach another device: no remote copies, remote signals or barrier semaphores. Data moves between devices by JAX's collectives and lax.ppermute only.
A program may use at most 128 MiB of HBM per device.

v0:
```python
import functools

import jax
import jax.numpy as jnp
from jax import lax
from jax.experimental import pallas as pl
from jax.experimental.pallas import tpu as pltpu
from jax.sharding import PartitionSpec as P

HEAD_DIM = 64
WINDOW = 512
SLOTS = 16
BF16 = jnp.bfloat16
F32 = jnp.float32
I32 = jnp.int32
MIB = 1024 * 1024
NO_COST = pl.CostEstimate(flops=1, bytes_accessed=1, transcendentals=0)


def cost(gflop):
    return pl.CostEstimate(flops=int(gflop * 10**9) + 1, bytes_accessed=MIB, transcendentals=0)


layer_eps = 1e-05
norm_eps = 1e-06

VMEM = pl.BlockSpec(memory_space=pltpu.VMEM)
SMEM = pl.BlockSpec(memory_space=pltpu.SMEM)
HBM = pl.BlockSpec(memory_space=pltpu.HBM)
ANY = pl.BlockSpec(memory_space=pl.ANY)


def layer_norm(values, gain, shift):
    centre = values - jnp.mean(values, axis=-1, keepdims=True)
    spread = jnp.mean(centre * centre, axis=-1, keepdims=True)
    return centre * lax.rsqrt(spread + layer_eps) * gain + shift


def in_hbm(array):
    return pltpu.with_memory_space_constraint(array, pltpu.HBM)


def swap(value, axis, mask):
    count = lax.axis_size(axis)
    return lax.ppermute(value, axis, [(i, i ^ mask) for i in range(count)])


def matmul(left, right):
    return jnp.dot(left, right, preferred_element_type=F32)


def params(mib):
    return pltpu.CompilerParams(vmem_limit_bytes=mib * MIB)


def after(value, *others):
    return lax.optimization_barrier((value,) + others)[0]


def load_kernel(states, w, w_out, mine, w_here, half, sems):
    part = half.shape[0]
    first = pl.multiple_of((lax.axis_index("req") & 1) * part, part)
    copies = [
        pltpu.make_async_copy(source, target, sems.at[number])
        for number, (source, target) in enumerate(
            (
                (w_out.at[pl.ds(first, part)], half),
                (states.at[lax.axis_index("tp") & 1], mine),
                (w, w_here),
            )
        )
    ]
    for copy in copies:
        copy.start()
    for copy in copies:
        copy.wait()


def load(states, w, w_out):
    return pl.pallas_call(
        load_kernel,
        out_shape=(
            jax.ShapeDtypeStruct(states.shape[1:], BF16),
            jax.ShapeDtypeStruct(w.shape, BF16),
            jax.ShapeDtypeStruct((w_out.shape[0] // 2, w_out.shape[1]), BF16),
        ),
        in_specs=[HBM] * 3,
        out_specs=(VMEM, VMEM, VMEM),
        scratch_shapes=[pltpu.SemaphoreType.DMA((3,))],
        compiler_params=params(6),
        cost_estimate=NO_COST,
        name="load",
    )(in_hbm(states), in_hbm(w), in_hbm(w_out))


def first_attention_kernel(lengths, mine, s1, s2, s3, w, b, out, text, parts, bias):
    core = lax.axis_index("tp") & 1
    text[...] = jnp.concatenate([mine[...], s1[core], s2[core], s3[core]])
    for which in range(3):
        project(which, text, w, b, parts)
    attend(lengths, parts, bias, out)


def second_attention_kernel(
    rows_here, lengths, text, w, b, i0, i1, out, numbers, place, rounds, parts, bias
):
    plan_rows(0, rows_here, (i0, i1), numbers, place, rounds)
    for which in range(3):
        project(which, text, w, b, parts)
    attend(lengths, parts, bias, out)


def project(which, text, w, b, parts):
    parts[which] = (matmul(text[...], w[which]) + b[which : which + 1, :]).astype(BF16)


def attend(lengths, parts, bias, out):
    rank = lax.axis_index("tp")
    length = lengths[rank & 1]
    _, seq_len, wide = parts.shape
    share = seq_len // 4

    def position(index):
        return ((index // share) ^ rank) * share + index % share

    row_pos = position(lax.broadcasted_iota(I32, (seq_len, 1), 0))
    col_pos = position(lax.broadcasted_iota(I32, (1, seq_len), 1))
    keep = (jnp.abs(row_pos - col_pos) <= WINDOW // 2) & (col_pos < length)
    bias[...] = jnp.where(keep, F32(0.0), F32(-1e30))
    ones = jnp.ones((seq_len, 128), BF16)
    low = lax.broadcasted_iota(I32, (1, 128), 1) < HEAD_DIM
    scale = jnp.asarray(HEAD_DIM**-0.5, BF16)
    for pair in range(wide // 128):
        lanes = slice(pair * 128, (pair + 1) * 128)
        k_pair = parts[1, :, lanes]
        v_ones = jnp.concatenate([parts[2, :, lanes], ones], axis=1)
        for block in range(4):
            rows = slice(block * share, (block + 1) * share)
            q_pair = parts[0, rows, lanes] * scale
            found = []
            for head in range(2):
                chosen = low if head == 0 else jnp.logical_not(low)
                q_head = jnp.where(chosen, q_pair, jnp.zeros((), BF16))
                logits = lax.dot_general(
                    q_head, k_pair, (((1,), (1,)), ((), ())), preferred_element_type=F32
                )
                logits = logits + bias[rows, :]
                top = jnp.max(logits, axis=-1, keepdims=True)
                expo = jnp.exp(logits - top).astype(BF16)
                summed = matmul(expo, v_ones)
                found.append(summed[:, :128] / summed[:, 128:])
            context = jnp.where(low, found[0], found[1])
            context = jnp.where(row_pos[rows] < length, context, F32(0.0))
            out[rows, lanes] = context.astype(BF16)


def attention_scratch(seq_len, wide):
    return [pltpu.VMEM((3, seq_len, wide), BF16), pltpu.VMEM((seq_len, seq_len), F32)]


def first_attention(lengths, blocks, w, b):
    share, width = blocks[0].shape
    wide = w.shape[2]
    return pl.pallas_call(
        first_attention_kernel,
        out_shape=(
            jax.ShapeDtypeStruct((4 * share, wide), BF16),
            jax.ShapeDtypeStruct((4 * share, width), BF16),
        ),
        in_specs=[SMEM] + [VMEM] * 6,
        out_specs=(VMEM, VMEM),
        scratch_shapes=attention_scratch(4 * share, wide),
        compiler_params=params(12),
        cost_estimate=NO_COST,
        name="attention_own",
    )(in_hbm(lengths), *blocks, w, in_hbm(b))


def second_attention(lengths, text, w, b, ids, rows_here):
    seq_len = text.shape[0]
    wide = w.shape[2]
    groups, each = ids[0].shape
    return pl.pallas_call(
        functools.partial(second_attention_kernel, rows_here),
        out_shape=(
            jax.ShapeDtypeStruct((seq_len, wide), BF16),
            jax.ShapeDtypeStruct((2, groups * SLOTS), I32),
            jax.ShapeDtypeStruct((groups * SLOTS, 2 * each), BF16),
            jax.ShapeDtypeStruct((1,), I32),
        ),
        in_specs=[SMEM] + [VMEM] * 5,
        out_specs=(VMEM, VMEM, VMEM, SMEM),
        scratch_shapes=attention_scratch(seq_len, wide),
        compiler_params=params(12),
        cost_estimate=cost(6),
        name="attention_partner",
    )(in_hbm(lengths), text, w, b, *ids)


def joined(first, second):
    swapped = (lax.axis_index("req") & 1) != 0
    low = jnp.where(swapped, second[...], first[...])
    high = jnp.where(swapped, first[...], second[...])
    return jnp.concatenate([low, high])


def project_first_kernel(
    text, here, w, b, numbers, index, out, keep, send,
    chosen, tiles, rows, sems, sem,
):
    copy = pltpu.make_async_copy(numbers, chosen, sem)
    copy.start()
    copy.wait()
    finish_rows = fetch_rows(chosen, index, tiles, rows, sems)
    out[...] = matmul(here[...], w[...]) + (text[...].astype(F32) + b[...])
    finish_rows(keep, send)


def project_first(text, here, w, b_out, numbers, index_rows):
    seq_len, width = text.shape
    slots = numbers.shape[1]
    half = jax.ShapeDtypeStruct((slots // 2, width), BF16)
    return pl.pallas_call(
        project_first_kernel,
        out_shape=(jax.ShapeDtypeStruct((seq_len, width), F32), half, half),
        in_specs=[VMEM] * 5 + [HBM],
        out_specs=(VMEM, VMEM, VMEM),
        scratch_shapes=fetch_scratch(slots, width),
        compiler_params=params(12 + slots // 16),
        cost_estimate=cost(1),
        name="project_first",
    )(text, here, w, b_out, numbers, in_hbm(index_rows))


def project_second_kernel(base, context, w, there, half_0, half_1, out):
    half = base.shape[0] // 2
    w_there = joined(half_0, half_1)
    for number in range(2):
        span = slice(number * half, (number + 1) * half)
        other = slice((1 - number) * half, (2 - number) * half)
        total = matmul(context[span, :], w[...]) + matmul(there[other, :], w_there)
        out[span, :] = base[span, :] + total


def project_second(base, context, w, there, halves):
    return pl.pallas_call(
        project_second_kernel,
        out_shape=jax.ShapeDtypeStruct(base.shape, F32),
        in_specs=[VMEM] * 6,
        out_specs=VMEM,
        input_output_aliases={0: 0},
        compiler_params=params(12),
        cost_estimate=cost(1),
        name="project_second",
    )(base, context, w, there, *halves)


def feed_kernel(
    keep_rest, base, c3, half_0, half_1, gain, shift, b0, b1, b_down,
    up_own, up_partner, down_own, down_partner, out, up_buf, down_buf, act, sems,
):
    hidden = up_own.shape[1]
    up_copy = pltpu.make_async_copy(up_own, up_buf, sems.at[0])
    down_copy = pltpu.make_async_copy(down_own, down_buf, sems.at[1])
    up_copy.start()
    down_copy.start()
    total = base[...] + matmul(c3[...], joined(half_0, half_1))
    normed = layer_norm(total, gain[...], shift[...]).astype(BF16)
    step = 512
    for part, (weight, bias) in enumerate(((up_partner, b1), (up_buf, b0))):
        if part == 1:
            up_copy.wait()
        for low in range(0, hidden, step):
            lanes = slice(low, low + step)
            up = matmul(normed, weight[:, lanes]) + bias[:, lanes]
            activated = 0.5 * up * (1.0 + lax.erf(up * F32(0.5**0.5)))
            act[:, part * hidden + low : part * hidden + low + step] = activated.astype(BF16)
    down = matmul(act[:, :hidden], down_partner[...])
    down_copy.wait()
    down = down + matmul(act[:, hidden:], down_buf[...])
    if keep_rest:
        down = down + (normed.astype(F32) + b_down[...])
    out[...] = down.astype(out.dtype)


def feed_forward(keep_rest, base, context, halves, gain, shift, biases, b_down, ups, downs):
    seq_len, width = base.shape
    half = seq_len // 2
    here = 0 if keep_rest else 1
    hidden = ups[0].shape[1]
    heads_wide = context.shape[1]
    base_spec = pl.BlockSpec((half, width), lambda i: (here, 0))
    context_spec = pl.BlockSpec((half, heads_wide), lambda i: (1 - here, 0))
    return pl.pallas_call(
        lambda *refs: feed_kernel(keep_rest, *refs),
        out_shape=jax.ShapeDtypeStruct((half, width), F32 if keep_rest else BF16),
        grid=(1,),
        in_specs=[base_spec, context_spec] + [VMEM] * 7
        + [HBM, VMEM, HBM, VMEM],
        out_specs=VMEM,
        scratch_shapes=[
            pltpu.VMEM((width, hidden), BF16),
            pltpu.VMEM((hidden, width), BF16),
            pltpu.VMEM((half, 2 * hidden), BF16),
            pltpu.SemaphoreType.DMA((2,)),
        ],
        compiler_params=params(20),
        cost_estimate=cost(8),
        name="feed_here" if keep_rest else "feed_there",
    )(base, context, *halves, gain, shift, *biases, b_down, in_hbm(ups[0]), ups[1],
      in_hbm(downs[0]), downs[1])


def finish_kernel(lengths, here, there, gain, shift, own, other, pool):
    rank = lax.axis_index("tp")
    length = lengths[rank & 1]
    share = own.shape[0]
    total = here[...] + there[...].astype(F32)
    hidden = layer_norm(total, gain[...], shift[...]).astype(BF16)
    own[...] = hidden[:share]
    other[...] = hidden[share:]
    index = lax.broadcasted_iota(I32, (2 * share, 1), 0)
    pos = ((index // share) ^ rank) * share + index % share
    valid = jnp.where(pos < length, hidden.astype(F32), F32(0.0))
    pool[...] = jnp.sum(valid, axis=0, keepdims=True)


def finish(lengths, here, there, gain, shift):
    half, width = here.shape
    block = jax.ShapeDtypeStruct((half // 2, width), BF16)
    return pl.pallas_call(
        finish_kernel,
        out_shape=(block, block, jax.ShapeDtypeStruct((1, width), F32)),
        in_specs=[SMEM] + [VMEM] * 4,
        out_specs=(VMEM, VMEM, VMEM),
        compiler_params=params(8),
        cost_estimate=cost(2),
        name="finish",
    )(lengths, here, there, gain, shift)


def score_kernel(
    lengths, pool, pool_core, pool_chip, pool_diag, rows, own, other, out, hidden_out
):
    core = lax.axis_index("tp") & 1
    width = pool.shape[1]
    mine = pool[...] + pool_chip[...]
    theirs = pool_core[...] + pool_diag[...]
    first = jnp.where(core == 0, mine, theirs) / lengths[0].astype(F32)
    second = jnp.where(core == 0, theirs, mine) / lengths[1].astype(F32)
    row = lax.broadcasted_iota(I32, (8, width), 0)
    pooled = jnp.where(row == 0, first, jnp.where(row == 1, second, F32(0.0)))
    scale = lax.rsqrt(jnp.mean(pooled * pooled, axis=-1, keepdims=True) + norm_eps)
    queries = (pooled * scale).astype(BF16)
    found = lax.dot_general(
        queries, rows[...], (((1,), (1,)), ((), ())), preferred_element_type=F32
    )
    each = rows.shape[0] // 2
    out[0:1, :] = found[0:1, :each]
    out[1:2, :] = found[1:2, each:]
    hidden_out[core] = own[...]
    hidden_out[1 - core] = other[...]


def score(lengths, pools, rows, own, other):
    return pl.pallas_call(
        score_kernel,
        out_shape=(
            jax.ShapeDtypeStruct((2, rows.shape[0] // 2), F32),
            jax.ShapeDtypeStruct((2,) + own.shape, BF16),
        ),
        in_specs=[SMEM] + [VMEM] * 7,
        out_specs=(VMEM, VMEM),
        compiler_params=params(8),
        cost_estimate=cost(1),
        name="score",
    )(lengths, *pools, rows, own, other)


def source_order(groups):
    order = [0]
    mask = groups // 2
    while mask >= 4:
        order = order + [entry + mask for entry in order]
        mask //= 2
    return [entry + last for last in range(4) for entry in order]


def as_ones(mask):
    return mask.astype(F32).astype(BF16)


def plan_rows(first_place, rows_here, parts, numbers, place, rounds):
    rank = lax.axis_index("tp")
    group = lax.axis_index("req")
    groups = parts[0].shape[0]
    slots = groups * SLOTS
    ids = jnp.concatenate([part[...] for part in parts], axis=1)
    count = ids.shape[1]
    owner = lax.shift_right_logical(ids, I32(rows_here.bit_length() - 1))
    before = as_ones(
        lax.broadcasted_iota(I32, (count, count), 0)
        < lax.broadcasted_iota(I32, (count, count), 1)
    )
    ones = jnp.ones((count, 128), BF16)
    slot = lax.broadcasted_iota(I32, (SLOTS, 1), 0) + first_place

    mine = owner == group * 4 + rank
    asked = jnp.concatenate(
        [
            (owner[:1] == (group ^ source) * 4 + rank).astype(F32)
            for source in source_order(groups)
        ]
    )
    both = jnp.concatenate([mine.astype(F32), asked]).astype(BF16)
    ranks = matmul(both, before).astype(I32)
    send_rank = jnp.where(mine, ranks[:groups], -1)
    take_rank = jnp.where(asked > 0, ranks[groups:], -1)

    local = jnp.where(mine, ids - (group * 4 + rank) * rows_here, 0)
    high = (local >> 6).astype(F32).astype(BF16)
    low = (local & 63).astype(F32).astype(BF16)
    chosen = jnp.concatenate(
        [(send_rank[k : k + 1] == slot).astype(F32) for k in range(groups)]
    ).astype(BF16)
    spread = (((1,), (1,)), ((), ()))
    wanted = 64.0 * lax.dot_general(high, chosen, spread, preferred_element_type=F32)
    wanted = wanted + lax.dot_general(low, chosen, spread, preferred_element_type=F32)
    counts = matmul(as_ones(mine), jnp.ones((count, slots), BF16))
    own = lax.broadcasted_iota(I32, (groups, slots), 0) == lax.div(
        lax.broadcasted_iota(I32, (groups, slots), 1), I32(SLOTS)
    )
    numbers[0:1, :] = jnp.sum(jnp.where(own, wanted, 0.0), axis=0, keepdims=True).astype(I32)
    counts = jnp.sum(jnp.where(own, counts, 0.0), axis=0, keepdims=True).astype(I32)
    numbers[1:2, :] = counts - first_place

    for k in range(groups):
        place[k * SLOTS : (k + 1) * SLOTS, :] = as_ones(take_rank[k : k + 1] == slot)
    shard = lax.broadcasted_iota(I32, (4 * groups, 1), 0)
    load = jnp.concatenate(
        [(owner[k : k + 1] == shard).astype(F32) for k in range(groups)]
    ).astype(BF16)
    most = jnp.max(matmul(load, ones)).astype(I32)
    rounds[0] = (most + SLOTS - 1) // SLOTS - 1


def fetch_rows(chosen, index, tiles, rows, sems):
    deep = tiles.shape[1]
    slots = tiles.shape[0]
    step = 4

    def tile_copy(slot):
        first = pl.multiple_of((chosen[0, slot] // deep) * deep, deep)
        return pltpu.make_async_copy(index.at[pl.ds(first, deep)], tiles.at[slot], sems.at[slot])

    def start(number, carry):
        for each in range(step):
            tile_copy(number * step + each).start()
        return carry

    def select(number, carry):
        for each in range(step):
            tile_copy(number * step + each).wait()
        for each in range(step):
            source = number * step + each
            line = lax.broadcasted_iota(I32, (deep, 1), 0) == chosen[0, source] % deep
            row = jnp.where(line, tiles[source].astype(F32), F32(0.0))
            rows[pl.ds(source, 1), :] = jnp.sum(row, axis=0, keepdims=True)
        return carry

    def each_group(action):
        def one(number, carry):
            first = number * (SLOTS // step)
            left = jnp.clip(chosen[1, number * SLOTS], 0, SLOTS)
            return lax.fori_loop(first, first + (left + step - 1) // step, action, carry)

        lax.fori_loop(0, slots // SLOTS, one, 0)

    rows[...] = jnp.zeros_like(rows)
    each_group(start)

    def finish_rows(keep, send):
        each_group(select)
        keep[...] = rows[: slots // 2, :].astype(BF16)
        send[...] = rows[slots // 2 :, :].astype(BF16)

    return finish_rows


def take_kernel(
    number, i0, i1, index, keep, send, place, rounds, numbers, chosen, tiles, rows,
    sems, sem,
):
    plan_rows(number[0] * SLOTS, index.shape[0], (i0, i1), numbers, place, rounds)
    copy = pltpu.make_async_copy(numbers, chosen, sem)
    copy.start()
    copy.wait()
    fetch_rows(chosen, index, tiles, rows, sems)(keep, send)


def fetch_scratch(slots, width):
    return [
        pltpu.SMEM((2, slots), I32),
        pltpu.VMEM((slots, 16, width), BF16),
        pltpu.VMEM((slots, width), F32),
        pltpu.SemaphoreType.DMA((slots,)),
        pltpu.SemaphoreType.DMA,
    ]


def take_rows(number, ids, index_rows):
    groups, each = ids[0].shape
    slots = groups * SLOTS
    width = index_rows.shape[1]
    half = jax.ShapeDtypeStruct((slots // 2, width), BF16)
    return pl.pallas_call(
        take_kernel,
        out_shape=(
            half,
            half,
            jax.ShapeDtypeStruct((slots, 2 * each), BF16),
            jax.ShapeDtypeStruct((1,), I32),
        ),
        in_specs=[SMEM] + [VMEM] * 2 + [HBM],
        out_specs=(VMEM, VMEM, VMEM, SMEM),
        scratch_shapes=[pltpu.VMEM((2, slots), I32)] + fetch_scratch(slots, width),
        compiler_params=params(8 + slots // 16),
        cost_estimate=NO_COST,
        name="take_rows",
    )(number, *ids, in_hbm(index_rows))


def place_kernel(place, h0, h1, h2, h3, out):
    received = jnp.concatenate([h0[...], h1[...], h2[...], h3[...]])
    chosen = lax.dot_general(
        place[...], received, (((0,), (0,)), ((), ())), preferred_element_type=F32
    )
    out[...] = chosen.astype(BF16)


def place_rows(place, received):
    return pl.pallas_call(
        place_kernel,
        out_shape=jax.ShapeDtypeStruct((place.shape[1], received[0].shape[1]), BF16),
        in_specs=[VMEM] * 5,
        out_specs=VMEM,
        compiler_params=params(8),
        cost_estimate=NO_COST,
        name="place_rows",
    )(place, *received)


def masks(axis):
    mask = 1
    while mask < lax.axis_size(axis):
        yield mask
        mask *= 2


def row_exchange(ids, index_rows, place, rounds):
    width = index_rows.shape[1]

    def gathered(keep, send, place, gates=((), (), ())):
        keep = keep.reshape(1, -1, SLOTS, width)
        send = send.reshape(1, -1, SLOTS, width)
        held = None
        for mask in list(masks("req"))[:1:-1]:
            if held is not None:
                keep, send = held[:, :mask], held[:, mask:]
            other = swap(send, "req", mask)
            if mask == 4:
                other = after(other, *gates[0])
            held = jnp.concatenate([keep, other])
        others = [swap(held[:, mask], "req", mask) for mask in (1, 2, 3)]
        others = list(after(tuple(others), *gates[1]))
        held = [part.reshape(-1, width) for part in [held[:, 0]] + others]
        found = place_rows(place, held)
        found = after(found, *gates[2]).reshape(4, -1, width)
        parts = [swap(found[place], "tp", mask) for place, mask in ((1, 2), (2, 1), (3, 3))]
        return found[0] + parts[0] + parts[1] + parts[2]

    def one_more(state):
        number, total = state
        keep, send, place, _ = take_rows(number.reshape(1), ids, index_rows)
        return number - 1, total + gathered(keep, send, place)

    def further(rows, *gate):
        left = after(rounds, *gate)[0]
        return lax.while_loop(lambda state: state[0] > 0, one_more, (left, rows))[1]

    return lambda keep, send, *gates: gathered(keep, send, place, gates), further


def per_device(
    states,
    lengths,
    w_qkv,
    b_qkv,
    w_out,
    b_out,
    ln1_gain,
    ln1_shift,
    w_up,
    b_up,
    w_down,
    b_down,
    ln2_gain,
    ln2_shift,
    index_rows,
    cand_ids,
):
    from_core = swap(states, "tp", 1)
    w_qkv_t = w_qkv.transpose(1, 0, 2)
    w_qkv_p = swap(w_qkv_t, "tp", 1)
    b_qkv_p = swap(b_qkv, "tp", 1)
    b_up_p = swap(b_up, "tp", 1)

    held = cand_ids.reshape(1, -1)
    held = jnp.concatenate([held, swap(held, "tp", 2)], axis=1)
    from_chip = swap(after(states, held), "tp", 2)
    for mask in masks("req"):
        other = swap(held, "req", mask)
        if mask * 2 == lax.axis_size("req"):
            mine, w_here, w_half = load(states, w_qkv_t, after(w_out, held))
            other, mine = lax.optimization_barrier((other, mine))
        held = jnp.concatenate([held, other])
    from_chip, held, from_core, w_qkv_p, b_qkv_p, b_up_p = lax.optimization_barrier(
        (from_chip, held, from_core, w_qkv_p, b_qkv_p, b_up_p)
    )
    w_out_p = swap(after(w_out, from_chip), "tp", 1)
    from_diag = swap(from_chip, "tp", 1)
    blocks = (mine, from_core, from_chip, from_diag)
    ids = (held, swap(held, "tp", 1))
    w_up_p = swap(after(w_up, from_diag, w_out_p, *ids), "tp", 1)
    w_down_p = swap(after(w_down, from_diag, w_out_p, *ids), "tp", 1)
    w_x0 = swap(w_half, "tp", 2)

    blocks, ids, w_out_p = lax.optimization_barrier((blocks, ids, w_out_p))
    context_0, text = first_attention(lengths, blocks, w_here, b_qkv)
    context_0x = swap(context_0, "tp", 2)
    context_1, numbers, place, rounds = second_attention(
        lengths, after(text, w_up_p), w_qkv_p, b_qkv_p, ids, index_rows.shape[0]
    )
    context_1x = swap(context_1, "tp", 2)
    w_x1 = swap(after(w_x0, context_1), "req", 1)
    w_d0 = swap(after(w_x0, context_1), "tp", 1)

    base, keep, send = project_first(
        text, after(context_0, context_0x), w_out, b_out[None], numbers, index_rows
    )
    w_d1 = swap(after(w_x1, base), "tp", 1)
    base = project_second(base, context_1, w_out_p, context_0x, (w_x0, w_x1))
    gathered, further = row_exchange(ids, index_rows, place, rounds)
    common = (
        context_1x, (w_d0, w_d1), ln1_gain[None], ln1_shift[None],
        (b_up[None], b_up_p[None]), b_down[None], (w_up, w_up_p),
        (w_down, w_down_p),
    )
    down_there = feed_forward(False, base, *common)
    down_x = swap(down_there, "tp", 2)
    down_here = feed_forward(True, after(base, down_there), *common)
    down_x = after(down_x, down_here)
    hidden, hidden_other, pool = finish(
        lengths, down_here, down_x, ln2_gain[None], ln2_shift[None]
    )

    rows = gathered(keep, send, (down_there,), (down_here,), ())
    pools = (pool,) + tuple(swap(pool, "tp", mask) for mask in (1, 2, 3))
    hidden_p = swap(hidden_other, "tp", 1)
    rows = further(after(rows, *pools), *pools)
    scores, hidden_out = score(lengths, pools, rows, hidden, hidden_p)
    return (hidden_out, scores)


def solution(mesh):
    placed = (
        P("req", "tp", None),
        P("req"),
        P(None, None, "tp"),
        P(None, "tp"),
        P("tp", None),
        P(),
        P(),
        P(),
        P(None, "tp"),
        P("tp"),
        P("tp", None),
        P(),
        P(),
        P(),
        P(("req", "tp"), None),
        P("req", "tp"),
    )
    return jax.shard_map(
        per_device,
        mesh=mesh,
        in_specs=placed,
        out_specs=(P("req", "tp", None), P("req", "tp")),
        check_vma=False,
    )
```

profile of v0, /device:TPU:0, one launch (start us, length us, event | category | flops | bytes accessed | tf_op | source)
XLA Modules:
  0.0 72.8 jit_solution(15154737963811158070)
XLA Ops:
  1.9 2.5 %collective-permute-start.7 = (s32[1,32]{1,0:T(1,128)S(1)}, s32[1,32]{1,0:T(1,128)S(1)}, u32[]{:S(2)}, u32[]{:S(2)}) collective-permute-start(s32[1,32]{1,0:T(1,128)S(1)} %reshape.64), channel_id=1, source_target_pairs={{0,2},{1,3},{2,0},{3,1},{4,6},{5,7},{6,4},{7,5},{8,10},{9,11},{10,... | collective-permute-start | bytes 392 | tf_op jit(solution)/shard_map/ppermute | solution.py:45
  4.7 1.3 %collective-permute-done.7 = s32[1,32]{1,0:T(1,128)S(1)} collective-permute-done((s32[1,32]{1,0:T(1,128)S(1)}, s32[1,32]{1,0:T(1,128)S(1)}, u32[]{:S(2)}, u32[]{:S(2)}) %collective-permute-start.7) | collective-permute-done | bytes 160 | tf_op jit(solution)/shard_map/ppermute | solution.py:45
  6.0 2.0 %collective-permute-start.11 = (bf16[2,128,1024]{2,1,0:T(8,128)(2,1)}, bf16[2,128,1024]{2,1,0:T(8,128)(2,1)S(1)}, u32[]{:S(2)}, u32[]{:S(2)}) collective-permute-start(bf16[2,128,1024]{2,1,0:T(8,128)(2,1)} %states.1), channel_id=1, source_target_pairs={{0,2},{1,3},{2,0},{3,1},{4,6},{5,7},{6,4},{7,5},{8,10},{9,11},{10,... | collective-permute-start | bytes 1572872 | tf_op jit(solution)/shard_map/ppermute | solution.py:45
  8.1 1.5 %collective-permute-start.8 = (s32[1,64]{1,0:T(1,128)S(1)}, s32[1,64]{1,0:T(1,128)S(1)}, u32[]{:S(2)}, u32[]{:S(2)}) collective-permute-start(s32[1,64]{1,0:T(1,128)S(1)} %pad_add_fusion.3), channel_id=1, source_target_pairs={{0,4},{4,0},{8,12},{12,8},{16,20},{20,16},{24,28},{28,24},{1,5},{5... | collective-permute-start | bytes 776 | tf_op jit(solution)/shard_map/ppermute | solution.py:45
  9.6 2.0 %collective-permute-done.8 = s32[1,64]{1,0:T(1,128)S(1)} collective-permute-done((s32[1,64]{1,0:T(1,128)S(1)}, s32[1,64]{1,0:T(1,128)S(1)}, u32[]{:S(2)}, u32[]{:S(2)}) %collective-permute-start.8) | collective-permute-done | bytes 288 | tf_op jit(solution)/shard_map/ppermute | solution.py:45
  11.7 1.6 %collective-permute-start.9 = (s32[2,64]{1,0:T(2,128)S(1)}, s32[2,64]{1,0:T(2,128)S(1)}, u32[]{:S(2)}, u32[]{:S(2)}) collective-permute-start(s32[2,64]{1,0:T(2,128)S(1)} %pad_add_fusion.2), channel_id=1, source_target_pairs={{0,8},{4,12},{8,0},{12,4},{16,24},{20,28},{24,16},{28,20},{1,9},{5... | collective-permute-start | bytes 1544 | tf_op jit(solution)/shard_map/ppermute | solution.py:45
  13.3 2.0 %collective-permute-done.9 = s32[2,64]{1,0:T(2,128)S(1)} collective-permute-done((s32[2,64]{1,0:T(2,128)S(1)}, s32[2,64]{1,0:T(2,128)S(1)}, u32[]{:S(2)}, u32[]{:S(2)}) %collective-permute-start.9) | collective-permute-done | bytes 544 | tf_op jit(solution)/shard_map/ppermute | solution.py:45
  15.3 2.6 %collective-permute-start.10 = (s32[4,64]{1,0:T(4,128)S(1)}, s32[4,64]{1,0:T(4,128)S(1)}, u32[]{:S(2)}, u32[]{:S(2)}) collective-permute-start(s32[4,64]{1,0:T(4,128)S(1)} %pad_add_fusion.1), channel_id=1, source_target_pairs={{0,16},{4,20},{8,24},{12,28},{16,0},{20,4},{24,8},{28,12},{1,17},{... | collective-permute-start | bytes 3080 | tf_op jit(solution)/shard_map/ppermute | solution.py:45
  17.9 1.6 %load.1 = (bf16[128,1024]{1,0:T(8,128)(2,1)S(1)}, bf16[3,1024,256]{2,1,0:T(8,128)(2,1)S(1)}, bf16[128,1024]{1,0:T(8,128)(2,1)S(1)}) custom-call(bf16[2,128,1024]{2,1,0:T(8,128)(2,1)} %states.1, bf16[3,1024,256]{2,1,0:T(8,128)(2,1)} %bitcast.85, bf16[256,1024]{1,0:T(8,128)(2,1)} %w.1), custom_call_target="tpu_custom_call" | custom-call | flops 1 | bytes 1 | tf_op jit(solution)/shard_map/load/pallas_call | solution.py:80
  21.9 1.8 %collective-permute-done.17.i1 = s32[8,64]{1,0:T(8,128)S(1)} collective-permute-done((s32[8,64]{1,0:T(8,128)S(1)}, s32[8,64]{1,0:T(8,128)S(1)}, u32[]{:S(2)}, u32[]{:S(2)}) %collective-permute-start.17) | collective-permute-done | bytes 2080 | tf_op jit(solution)/shard_map/ppermute | solution.py:45
  24.8 4.2 %attention_own.1 = (bf16[512,256]{1,0:T(8,128)(2,1)S(1)}, bf16[512,1024]{1,0:T(8,128)(2,1)S(1)}) custom-call(s32[2]{0:T(128)} %lengths.7, bf16[128,1024]{1,0:T(8,128)(2,1)S(1)} %get-tuple-element.128.mine, bf16[2,128,1024]{2,1,0:T(8,128)(2,1)S(1)} %collective-permute-done.12.s1, bf16[2,128,1024]{2,1,0:T(8,128)(2,1)S(1)} %collective-permute-done.11.s2, ...), custom_call_target="tpu_custom_call" | custom-call | flops 1 | bytes 1 | tf_op jit(solution)/shard_map/attention_own/pallas_call | solution.py:164
  29.0 1.6 %collective-permute-start.19 = (bf16[512,256]{1,0:T(8,128)(2,1)S(1)}, bf16[512,256]{1,0:T(8,128)(2,1)S(1)}, u32[]{:S(2)}, u32[]{:S(2)}) collective-permute-start(bf16[512,256]{1,0:T(8,128)(2,1)S(1)} %get-tuple-element.135.here), channel_id=1, source_target_pairs={{0,2},{1,3},{2,0},{3,1},{4,6},{5,7},{6,4},{7,5},{8,10},{9,11},{10,... | collective-permute-start | bytes 786440 | tf_op jit(solution)/shard_map/ppermute | solution.py:45
  30.6 5.0 %attention_partner.1 = (bf16[512,256]{1,0:T(8,128)(2,1)S(1)}, s32[2,128]{1,0:T(2,128)S(1)}, bf16[128,128]{1,0:T(8,128)(2,1)S(1)}, s32[1]{0:T(128)}) custom-call(s32[2]{0:T(128)} %lengths.7, bf16[512,1024]{1,0:T(8,128)(2,1)S(1)} %get-tuple-element.137.text, bf16[3,1024,256]{2,1,0:T(8,128)(2,1)S(1)} %collective-permute-done.13.w, ...), custom_call_target="tpu_custom_call" | custom-call | flops 6000000000 | bytes 1048576 | tf_op jit(solution)/shard_map/attention_partner/pallas_call | solution.py:183
  35.6 1.6 %collective-permute-start.22 = (bf16[128,1024]{1,0:T(8,128)(2,1)S(1)}, bf16[128,1024]{1,0:T(8,128)(2,1)S(1)}, u32[]{:S(2)}, u32[]{:S(2)}) collective-permute-start(bf16[128,1024]{1,0:T(8,128)(2,1)S(1)} %collective-permute-done.21.half_0), channel_id=1, source_target_pairs={{0,4},{4,0},{8,12},{12,8},{16,20},{20,16},{24,28},{28,24},{1,5},{5... | collective-permute-start | bytes 786440 | tf_op jit(solution)/shard_map/ppermute | solution.py:45
  39.0 4.0 %project_first.1 = (f32[512,1024]{1,0:T(8,128)S(1)}, bf16[64,1024]{1,0:T(8,128)(2,1)S(1)}, bf16[64,1024]{1,0:T(8,128)(2,1)S(1)}) custom-call(bf16[512,1024]{1,0:T(8,128)(2,1)S(1)} %get-tuple-element.137.text, bf16[512,256]{1,0:T(8,128)(2,1)S(1)} %get-tuple-element.135.here, bf16[256,1024]{1,0:T(8,128)(2,1)S(1)} %copy-done, f32[1,1024]{1,0:T(1,128)S(1)} %bitcast.69, ...), custom_call_target="tpu_custom_call" | custom-call | flops 1000000000 | bytes 1048576 | tf_op jit(solution)/shard_map/project_first/pallas_call | solution.py:223
  44.5 2.5 %collective-permute-start.31 = (bf16[1,4,16,1024]{3,2,0,1:T(8,128)(2,1)S(1)}, bf16[1,4,16,1024]{3,2,0,1:T(8,128)(2,1)S(1)}, u32[]{:S(2)}, u32[]{:S(2)}) collective-permute-start(bf16[1,4,16,1024]{3,2,0,1:T(8,128)(2,1)S(1)} %bitcast.70), channel_id=1, source_target_pairs={{0,16},{4,20},{8,24},{12,28},{16,0},{20,4},{24,8},{28,12},{1,17},{... | collective-permute-start | bytes 393224 | tf_op jit(solution)/shard_map/ppermute | solution.py:45
  47.2 3.8 %feed_there.1 = bf16[256,1024]{1,0:T(8,128)(2,1)S(1)} custom-call(f32[512,1024]{1,0:T(8,128)S(1)} %project_second.1.refs_0_, bf16[512,256]{1,0:T(8,128)(2,1)S(1)} %collective-permute-done.23.refs_1_, bf16[128,1024]{1,0:T(8,128)(2,1)S(1)} %collective-permute-done.24.refs_2_, bf16[128,1024]{1,0:T(8,128)(2,1)S(1)} %collective-permute-done.25.refs_3_, ...), custom_call_target="tpu_custom_call" | custom-call | flops 8000000000 | bytes 1048576 | tf_op jit(solution)/shard_map/feed_there/pallas_call | solution.py:294
  51.9 2.3 %collective-permute-done.31 = bf16[1,4,16,1024]{3,2,0,1:T(8,128)(2,1)S(1)} collective-permute-done((bf16[1,4,16,1024]{3,2,0,1:T(8,128)(2,1)S(1)}, bf16[1,4,16,1024]{3,2,0,1:T(8,128)(2,1)S(1)}, u32[]{:S(2)}, u32[]{:S(2)}) %collective-permute-start.31) | collective-permute-done | bytes 131104 | tf_op jit(solution)/shard_map/ppermute | solution.py:45
  54.2 1.6 %collective-permute-start.34 = (bf16[2,16,1024]{2,1,0:T(8,128)(2,1)S(1)}, bf16[2,16,1024]{2,1,0:T(8,128)(2,1)S(1)}, u32[]{:S(2)}, u32[]{:S(2)}) collective-permute-start(bf16[2,16,1024]{2,1,0:T(8,128)(2,1)S(1)} %get-tuple-element.189), channel_id=1, source_target_pairs={{0,12},{4,8},{8,4},{12,0},{16,28},{20,24},{24,20},{28,16},{1,13},{... | collective-permute-start | bytes 196616 | tf_op jit(solution)/shard_map/ppermute | solution.py:45
  56.3 1.5 %collective-permute-start.33 = (bf16[2,16,1024]{2,1,0:T(8,128)(2,1)S(1)}, bf16[2,16,1024]{2,1,0:T(8,128)(2,1)S(1)}, u32[]{:S(2)}, u32[]{:S(2)}) collective-permute-start(bf16[2,16,1024]{2,1,0:T(8,128)(2,1)S(1)} %get-tuple-element.192), channel_id=1, source_target_pairs={{0,8},{4,12},{8,0},{12,4},{16,24},{20,28},{24,16},{28,20},{1,9},{5... | collective-permute-start | bytes 196616 | tf_op jit(solution)/shard_map/ppermute | solution.py:45
  57.8 3.8 %feed_here.1.here = f32[256,1024]{1,0:T(8,128)S(1)} custom-call(f32[512,1024]{1,0:T(8,128)S(1)} %project_second.1.refs_0_, bf16[512,256]{1,0:T(8,128)(2,1)S(1)} %collective-permute-done.23.refs_1_, bf16[128,1024]{1,0:T(8,128)(2,1)S(1)} %collective-permute-done.24.refs_2_, bf16[128,1024]{1,0:T(8,128)(2,1)S(1)} %collective-permute-done.25.refs_3_, ...), custom_call_target="tpu_custom_call" | custom-call | flops 8000000000 | bytes 1048576 | tf_op jit(solution)/shard_map/feed_here/pallas_call | solution.py:294
  62.7 1.4 %collective-permute-start.36 = (bf16[32,1024]{1,0:T(8,128)(2,1)S(1)}, bf16[32,1024]{1,0:T(8,128)(2,1)S(1)}, u32[]{:S(2)}, u32[]{:S(2)}) collective-permute-start(bf16[32,1024]{1,0:T(8,128)(2,1)S(1)} %get-tuple-element.188), channel_id=1, source_target_pairs={{0,1},{1,0},{2,3},{3,2},{4,5},{5,4},{6,7},{7,6},{8,9},{9,8},{10,11... | collective-permute-start | bytes 196616 | tf_op jit(solution)/shard_map/ppermute | solution.py:45
  64.1 1.6 %collective-permute-done.27.there = bf16[256,1024]{1,0:T(8,128)(2,1)S(1)} collective-permute-done((bf16[256,1024]{1,0:T(8,128)(2,1)S(1)}, bf16[256,1024]{1,0:T(8,128)(2,1)S(1)}, u32[]{:S(2)}, u32[]{:S(2)}) %collective-permute-start.27) | collective-permute-done | bytes 524320 | tf_op jit(solution)/shard_map/ppermute | solution.py:45
  71.2 1.6 %score.1 = (f32[2,16]{1,0:T(2,128)}, bf16[2,128,1024]{2,1,0:T(8,128)(2,1)}) custom-call(s32[2]{0:T(128)S(1)} %copy-done.2, f32[1,1024]{1,0:T(1,128)S(1)} %get-tuple-element.153.pool, f32[1,1024]{1,0:T(1,128)S(1)} %collective-permute-done.28.pool_core, f32[1,1024]{1,0:T(1,128)S(1)} %collective-permute-done.29.pool_chip, ...), custom_call_target="tpu_custom_call" | custom-call | flops 1000000000 | bytes 1048576 | tf_op jit(solution)/shard_map/score/pallas_call | solution.py:366
  (81 shorter events, 16.5 us)
Async XLA Ops:
  0.7 20.3 %collective-permute-start.13 = (bf16[3,1024,256]{2,1,0:T(8,128)(2,1)}, bf16[3,1024,256]{2,1,0:T(8,128)(2,1)S(1)}, u32[]{:S(2)}, u32[]{:S(2)}) collective-permute-start(bf16[3,1024,256]{2,1,0:T(8,128)(2,1)} %bitcast.84), channel_id=1, source_target_pairs={{0,1},{1,0},{2,3},{3,2},{4,5},{5,4},{6,7},{7,6},{8,9},{9,8},{10,11... | collective-permute-start | bytes 4718600 | tf_op jit(solution)/shard_map/ppermute | solution.py:45
  1.9 4.0 %collective-permute-start.7 = (s32[1,32]{1,0:T(1,128)S(1)}, s32[1,32]{1,0:T(1,128)S(1)}, u32[]{:S(2)}, u32[]{:S(2)}) collective-permute-start(s32[1,32]{1,0:T(1,128)S(1)} %reshape.64), channel_id=1, source_target_pairs={{0,2},{1,3},{2,0},{3,1},{4,6},{5,7},{6,4},{7,5},{8,10},{9,11},{10,... | collective-permute-start | bytes 392 | tf_op jit(solution)/shard_map/ppermute | solution.py:45
  4.4 16.5 %collective-permute-start.12 = (bf16[2,128,1024]{2,1,0:T(8,128)(2,1)}, bf16[2,128,1024]{2,1,0:T(8,128)(2,1)S(1)}, u32[]{:S(2)}, u32[]{:S(2)}) collective-permute-start(bf16[2,128,1024]{2,1,0:T(8,128)(2,1)} %states.1), channel_id=1, source_target_pairs={{0,1},{1,0},{2,3},{3,2},{4,5},{5,4},{6,7},{7,6},{8,9},{9,8},{10,11... | collective-permute-start | bytes 1572872 | tf_op jit(solution)/shard_map/ppermute | solution.py:45
  6.0 14.9 %collective-permute-start.11 = (bf16[2,128,1024]{2,1,0:T(8,128)(2,1)}, bf16[2,128,1024]{2,1,0:T(8,128)(2,1)S(1)}, u32[]{:S(2)}, u32[]{:S(2)}) collective-permute-start(bf16[2,128,1024]{2,1,0:T(8,128)(2,1)} %states.1), channel_id=1, source_target_pairs={{0,2},{1,3},{2,0},{3,1},{4,6},{5,7},{6,4},{7,5},{8,10},{9,11},{10,... | collective-permute-start | bytes 1572872 | tf_op jit(solution)/shard_map/ppermute | solution.py:45
  8.1 3.5 %collective-permute-start.8 = (s32[1,64]{1,0:T(1,128)S(1)}, s32[1,64]{1,0:T(1,128)S(1)}, u32[]{:S(2)}, u32[]{:S(2)}) collective-permute-start(s32[1,64]{1,0:T(1,128)S(1)} %pad_add_fusion.3), channel_id=1, source_target_pairs={{0,4},{4,0},{8,12},{12,8},{16,20},{20,16},{24,28},{28,24},{1,5},{5... | collective-permute-start | bytes 776 | tf_op jit(solution)/shard_map/ppermute | solution.py:45
  11.7 3.6 %collective-permute-start.9 = (s32[2,64]{1,0:T(2,128)S(1)}, s32[2,64]{1,0:T(2,128)S(1)}, u32[]{:S(2)}, u32[]{:S(2)}) collective-permute-start(s32[2,64]{1,0:T(2,128)S(1)} %pad_add_fusion.2), channel_id=1, source_target_pairs={{0,8},{4,12},{8,0},{12,4},{16,24},{20,28},{24,16},{28,20},{1,9},{5... | collective-permute-start | bytes 1544 | tf_op jit(solution)/shard_map/ppermute | solution.py:45
  15.3 4.5 %collective-permute-start.10 = (s32[4,64]{1,0:T(4,128)S(1)}, s32[4,64]{1,0:T(4,128)S(1)}, u32[]{:S(2)}, u32[]{:S(2)}) collective-permute-start(s32[4,64]{1,0:T(4,128)S(1)} %pad_add_fusion.1), channel_id=1, source_target_pairs={{0,16},{4,20},{8,24},{12,28},{16,0},{20,4},{24,8},{28,12},{1,17},{... | collective-permute-start | bytes 3080 | tf_op jit(solution)/shard_map/ppermute | solution.py:45
  23.7 6.9 %collective-permute-start.20 = (bf16[1024,1024]{1,0:T(8,128)(2,1)S(1)}, bf16[1024,1024]{1,0:T(8,128)(2,1)S(1)}, u32[]{:S(2)}, u32[]{:S(2)}) collective-permute-start(bf16[1024,1024]{1,0:T(8,128)(2,1)S(1)} %copy-done.10), channel_id=1, source_target_pairs={{0,1},{1,0},{2,3},{3,2},{4,5},{5,4},{6,7},{7,6},{8,9},{9,8},{10,11... | collective-permute-start | bytes 6291464 | tf_op jit(solution)/shard_map/ppermute | solution.py:45
  24.1 22.9 %collective-permute-start.26 = (bf16[1024,1024]{1,0:T(8,128)(2,1)}, bf16[1024,1024]{1,0:T(8,128)(2,1)S(1)}, u32[]{:S(2)}, u32[]{:S(2)}) collective-permute-start(bf16[1024,1024]{1,0:T(8,128)(2,1)} %refs_11_.3), channel_id=1, source_target_pairs={{0,1},{1,0},{2,3},{3,2},{4,5},{5,4},{6,7},{7,6},{8,9},{9,8},{10,11... | collective-permute-start | bytes 6291464 | tf_op jit(solution)/shard_map/ppermute | solution.py:45
  24.3 11.3 %collective-permute-start.21 = (bf16[128,1024]{1,0:T(8,128)(2,1)S(1)}, bf16[128,1024]{1,0:T(8,128)(2,1)S(1)}, u32[]{:S(2)}, u32[]{:S(2)}) collective-permute-start(bf16[128,1024]{1,0:T(8,128)(2,1)S(1)} %get-tuple-element.146), channel_id=1, source_target_pairs={{0,2},{1,3},{2,0},{3,1},{4,6},{5,7},{6,4},{7,5},{8,10},{9,11},{10,... | collective-permute-start | bytes 786440 | tf_op jit(solution)/shard_map/ppermute | solution.py:45
  29.0 9.4 %collective-permute-start.19 = (bf16[512,256]{1,0:T(8,128)(2,1)S(1)}, bf16[512,256]{1,0:T(8,128)(2,1)S(1)}, u32[]{:S(2)}, u32[]{:S(2)}) collective-permute-start(bf16[512,256]{1,0:T(8,128)(2,1)S(1)} %get-tuple-element.135.here), channel_id=1, source_target_pairs={{0,2},{1,3},{2,0},{3,1},{4,6},{5,7},{6,4},{7,5},{8,10},{9,11},{10,... | collective-permute-start | bytes 786440 | tf_op jit(solution)/shard_map/ppermute | solution.py:45
  35.6 8.0 %collective-permute-start.22 = (bf16[128,1024]{1,0:T(8,128)(2,1)S(1)}, bf16[128,1024]{1,0:T(8,128)(2,1)S(1)}, u32[]{:S(2)}, u32[]{:S(2)}) collective-permute-start(bf16[128,1024]{1,0:T(8,128)(2,1)S(1)} %collective-permute-done.21.half_0), channel_id=1, source_target_pairs={{0,4},{4,0},{8,12},{12,8},{16,20},{20,16},{24,28},{28,24},{1,5},{5... | collective-permute-start | bytes 786440 | tf_op jit(solution)/shard_map/ppermute | solution.py:45
  38.5 8.5 %collective-permute-start.24 = (bf16[128,1024]{1,0:T(8,128)(2,1)S(1)}, bf16[128,1024]{1,0:T(8,128)(2,1)S(1)}, u32[]{:S(2)}, u32[]{:S(2)}) collective-permute-start(bf16[128,1024]{1,0:T(8,128)(2,1)S(1)} %collective-permute-done.21.half_0), channel_id=1, source_target_pairs={{0,1},{1,0},{2,3},{3,2},{4,5},{5,4},{6,7},{7,6},{8,9},{9,8},{10,11... | collective-permute-start | bytes 786440 | tf_op jit(solution)/shard_map/ppermute | solution.py:45
  38.5 8.7 %collective-permute-start.23 = (bf16[512,256]{1,0:T(8,128)(2,1)S(1)}, bf16[512,256]{1,0:T(8,128)(2,1)S(1)}, u32[]{:S(2)}, u32[]{:S(2)}) collective-permute-start(bf16[512,256]{1,0:T(8,128)(2,1)S(1)} %get-tuple-element.144.context), channel_id=1, source_target_pairs={{0,2},{1,3},{2,0},{3,1},{4,6},{5,7},{6,4},{7,5},{8,10},{9,11},{10,... | collective-permute-start | bytes 786440 | tf_op jit(solution)/shard_map/ppermute | solution.py:45
  43.7 3.5 %collective-permute-start.25 = (bf16[128,1024]{1,0:T(8,128)(2,1)S(1)}, bf16[128,1024]{1,0:T(8,128)(2,1)S(1)}, u32[]{:S(2)}, u32[]{:S(2)}) collective-permute-start(bf16[128,1024]{1,0:T(8,128)(2,1)S(1)} %collective-permute-done.22.half_1), channel_id=1, source_target_pairs={{0,1},{1,0},{2,3},{3,2},{4,5},{5,4},{6,7},{7,6},{8,9},{9,8},{10,11... | collective-permute-start | bytes 786440 | tf_op jit(solution)/shard_map/ppermute | solution.py:45
  44.5 9.7 %collective-permute-start.31 = (bf16[1,4,16,1024]{3,2,0,1:T(8,128)(2,1)S(1)}, bf16[1,4,16,1024]{3,2,0,1:T(8,128)(2,1)S(1)}, u32[]{:S(2)}, u32[]{:S(2)}) collective-permute-start(bf16[1,4,16,1024]{3,2,0,1:T(8,128)(2,1)S(1)} %bitcast.70), channel_id=1, source_target_pairs={{0,16},{4,20},{8,24},{12,28},{16,0},{20,4},{24,8},{28,12},{1,17},{... | collective-permute-start | bytes 393224 | tf_op jit(solution)/shard_map/ppermute | solution.py:45
  51.0 14.7 %collective-permute-start.27 = (bf16[256,1024]{1,0:T(8,128)(2,1)S(1)}, bf16[256,1024]{1,0:T(8,128)(2,1)S(1)}, u32[]{:S(2)}, u32[]{:S(2)}) collective-permute-start(bf16[256,1024]{1,0:T(8,128)(2,1)S(1)} %feed_there.1), channel_id=1, source_target_pairs={{0,2},{1,3},{2,0},{3,1},{4,6},{5,7},{6,4},{7,5},{8,10},{9,11},{10,... | collective-permute-start | bytes 1572872 | tf_op jit(solution)/shard_map/ppermute | solution.py:45
  54.2 7.4 %collective-permute-start.34 = (bf16[2,16,1024]{2,1,0:T(8,128)(2,1)S(1)}, bf16[2,16,1024]{2,1,0:T(8,128)(2,1)S(1)}, u32[]{:S(2)}, u32[]{:S(2)}) collective-permute-start(bf16[2,16,1024]{2,1,0:T(8,128)(2,1)S(1)} %get-tuple-element.189), channel_id=1, source_target_pairs={{0,12},{4,8},{8,4},{12,0},{16,28},{20,24},{24,20},{28,16},{1,13},{... | collective-permute-start | bytes 196616 | tf_op jit(solution)/shard_map/ppermute | solution.py:45
  55.8 5.8 %collective-permute-start.32 = (bf16[2,16,1024]{2,1,0:T(8,128)(2,1)S(1)}, bf16[2,16,1024]{2,1,0:T(8,128)(2,1)S(1)}, u32[]{:S(2)}, u32[]{:S(2)}) collective-permute-start(bf16[2,16,1024]{2,1,0:T(8,128)(2,1)S(1)} %get-tuple-element.191), channel_id=1, source_target_pairs={{0,4},{4,0},{8,12},{12,8},{16,20},{20,16},{24,28},{28,24},{1,5},{5... | collective-permute-start | bytes 196616 | tf_op jit(solution)/shard_map/ppermute | solution.py:45
  56.3 5.3 %collective-permute-start.33 = (bf16[2,16,1024]{2,1,0:T(8,128)(2,1)S(1)}, bf16[2,16,1024]{2,1,0:T(8,128)(2,1)S(1)}, u32[]{:S(2)}, u32[]{:S(2)}) collective-permute-start(bf16[2,16,1024]{2,1,0:T(8,128)(2,1)S(1)} %get-tuple-element.192), channel_id=1, source_target_pairs={{0,8},{4,12},{8,0},{12,4},{16,24},{20,28},{24,16},{28,20},{1,9},{5... | collective-permute-start | bytes 196616 | tf_op jit(solution)/shard_map/ppermute | solution.py:45
  61.9 6.0 %collective-permute-start.35 = (bf16[32,1024]{1,0:T(8,128)(2,1)S(1)}, bf16[32,1024]{1,0:T(8,128)(2,1)S(1)}, u32[]{:S(2)}, u32[]{:S(2)}) collective-permute-start(bf16[32,1024]{1,0:T(8,128)(2,1)S(1)} %get-tuple-element.186), channel_id=1, source_target_pairs={{0,2},{1,3},{2,0},{3,1},{4,6},{5,7},{6,4},{7,5},{8,10},{9,11},{10,... | collective-permute-start | bytes 196616 | tf_op jit(solution)/shard_map/ppermute | solution.py:45
  62.7 6.0 %collective-permute-start.37 = (bf16[32,1024]{1,0:T(8,128)(2,1)S(1)}, bf16[32,1024]{1,0:T(8,128)(2,1)S(1)}, u32[]{:S(2)}, u32[]{:S(2)}) collective-permute-start(bf16[32,1024]{1,0:T(8,128)(2,1)S(1)} %get-tuple-element.187), channel_id=1, source_target_pairs={{0,3},{1,2},{2,1},{3,0},{4,7},{5,6},{6,5},{7,4},{8,11},{9,10},{10,... | collective-permute-start | bytes 196616 | tf_op jit(solution)/shard_map/ppermute | solution.py:45
  62.7 6.0 %collective-permute-start.36 = (bf16[32,1024]{1,0:T(8,128)(2,1)S(1)}, bf16[32,1024]{1,0:T(8,128)(2,1)S(1)}, u32[]{:S(2)}, u32[]{:S(2)}) collective-permute-start(bf16[32,1024]{1,0:T(8,128)(2,1)S(1)} %get-tuple-element.188), channel_id=1, source_target_pairs={{0,1},{1,0},{2,3},{3,2},{4,5},{5,4},{6,7},{7,6},{8,9},{9,8},{10,11... | collective-permute-start | bytes 196616 | tf_op jit(solution)/shard_map/ppermute | solution.py:45
  66.9 3.7 %collective-permute-start.29 = (f32[1,1024]{1,0:T(1,128)S(1)}, f32[1,1024]{1,0:T(1,128)S(1)}, u32[]{:S(2)}, u32[]{:S(2)}) collective-permute-start(f32[1,1024]{1,0:T(1,128)S(1)} %get-tuple-element.153.pool), channel_id=1, source_target_pairs={{0,2},{1,3},{2,0},{3,1},{4,6},{5,7},{6,4},{7,5},{8,10},{9,11},{10,... | collective-permute-start | bytes 12296 | tf_op jit(solution)/shard_map/ppermute | solution.py:45
  (19 other events, 145.4 us)
where the time goes:
time: 73.2 us; the launch traced here: 72.8 us
  starting transfers between devices  28.1 us (38%)
  Pallas kernels  26.2 us (36%)
  waiting for transfers between devices  15.8 us (22%)
  between operations  0.88 us (1%)
  local copies, waits for them, and re-layouts  0.82 us (1%)
    ppermute x32, starting transfers between devices, swap(): return lax.ppermute(value, axis, [(i, i ^ mask) for i in range(count)])  28.1 us
    ppermute x32, waiting for transfers between devices, swap(): return lax.ppermute(value, axis, [(i, i ^ mask) for i in range(count)])  15.8 us
    pallas_call x2, Pallas kernels, feed_forward(): pl.pallas_call(lambda *refs: feed_kernel(keep_rest, *refs), out_shape=jax...  7.61 us
    pallas_call x1, Pallas kernels, second_attention(): pl.pallas_call(functools.partial(second_attention_kernel, rows_here), out...  4.96 us
    pallas_call x1, Pallas kernels, first_attention(): pl.pallas_call(first_attention_kernel, out_shape=(jax.ShapeDtypeStruct((4...  4.21 us
    pallas_call x1, Pallas kernels, project_first(): pl.pallas_call(project_first_kernel, out_shape=(jax.ShapeDtypeStruct((seq...  4.05 us
    pallas_call x1, Pallas kernels, load(): pl.pallas_call(load_kernel, out_shape=(jax.ShapeDtypeStruct(states.shape[...  1.61 us
    pallas_call x1, Pallas kernels, score(): pl.pallas_call(score_kernel, out_shape=(jax.ShapeDtypeStruct((2, rows.sha...  1.59 us
  transfers between devices with their start and end apart: 32, of which 14 were waited for; matrix products, arithmetic and copies ran while one was open for 2% of the time, Pallas kernels for 34%

commit v1 on v0

--- a/solution.py
+++ b/solution.py
@@ -137,19 +137,20 @@
         for block in range(4):
             rows = slice(block * share, (block + 1) * share)
             q_pair = parts[0, rows, lanes] * scale
-            found = []
-            for head in range(2):
-                chosen = low if head == 0 else jnp.logical_not(low)
-                q_head = jnp.where(chosen, q_pair, jnp.zeros((), BF16))
-                logits = lax.dot_general(
-                    q_head, k_pair, (((1,), (1,)), ((), ())), preferred_element_type=F32
-                )
-                logits = logits + bias[rows, :]
-                top = jnp.max(logits, axis=-1, keepdims=True)
-                expo = jnp.exp(logits - top).astype(BF16)
-                summed = matmul(expo, v_ones)
-                found.append(summed[:, :128] / summed[:, 128:])
-            context = jnp.where(low, found[0], found[1])
+            zero = jnp.zeros((), BF16)
+            q_heads = jnp.concatenate(
+                [jnp.where(low, q_pair, zero), jnp.where(low, zero, q_pair)]
+            )
+            logits = lax.dot_general(
+                q_heads, k_pair, (((1,), (1,)), ((), ())), preferred_element_type=F32
+            )
+            masked = bias[rows, :]
+            logits = logits + jnp.concatenate([masked, masked])
+            top = jnp.max(logits, axis=-1, keepdims=True)
+            expo = jnp.exp(logits - top).astype(BF16)
+            summed = matmul(expo, v_ones)
+            found = summed[:, :128] / summed[:, 128:]
+            context = jnp.where(low, found[:share], found[share:])
             context = jnp.where(row_pos[rows] < length, context, F32(0.0))
             out[rows, lanes] = context.astype(BF16)
 
@@ -643,11 +644,11 @@
     )
     context_1x = swap(context_1, "tp", 2)
     w_x1 = swap(after(w_x0, context_1), "req", 1)
-    w_d0 = swap(after(w_x0, context_1), "tp", 1)
 
     base, keep, send = project_first(
         text, after(context_0, context_0x), w_out, b_out[None], numbers, index_rows
     )
+    w_d0 = swap(after(w_x0, base), "tp", 1)
     w_d1 = swap(after(w_x1, base), "tp", 1)
     base = project_second(base, context_1, w_out_p, context_0x, (w_x0, w_x1))
     gathered, further = row_exchange(ids, index_rows, place, rounds)

time: 73.2 us -> 72.9 us (level)
  Pallas kernels: 26.2 us -> 24.8 us
  starting transfers between devices: 28.1 us -> 29.5 us
    ppermute x32, starting transfers between devices: 28.1 us -> 29.5 us  [swap(): return lax.ppermute(value, axis, [(i, i ^ mask) for i in range(count)])]
  transfers between devices with their start and end apart: 32 -> 32, of which waited for: 14 -> 12; matrix products, arithmetic and copies ran while one was open for 2% -> 2% of each run, Pallas kernels for 34% -> 32%
where the time goes in v1:
time: 72.9 us; the launch traced here: 72.6 us
  starting transfers between devices  29.5 us (40%)
  Pallas kernels  24.8 us (34%)
  waiting for transfers between devices  15.6 us (21%)
  between operations  0.93 us (1%)
  local copies, waits for them, and re-layouts  0.83 us (1%)
    ppermute x32, starting transfers between devices, swap(): return lax.ppermute(value, axis, [(i, i ^ mask) for i in range(count)])  29.5 us
    ppermute x32, waiting for transfers between devices, swap(): return lax.ppermute(value, axis, [(i, i ^ mask) for i in range(count)])  15.6 us
    pallas_call x2, Pallas kernels, feed_forward(): pl.pallas_call(lambda *refs: feed_kernel(keep_rest, *refs), out_shape=jax...  7.62 us
    pallas_call x1, Pallas kernels, second_attention(): pl.pallas_call(functools.partial(second_attention_kernel, rows_here), out...  4.4 us
    pallas_call x1, Pallas kernels, project_first(): pl.pallas_call(project_first_kernel, out_shape=(jax.ShapeDtypeStruct((seq...  3.75 us
    pallas_call x1, Pallas kernels, first_attention(): pl.pallas_call(first_attention_kernel, out_shape=(jax.ShapeDtypeStruct((4...  3.72 us
    pallas_call x1, Pallas kernels, load(): pl.pallas_call(load_kernel, out_shape=(jax.ShapeDtypeStruct(states.shape[...  1.61 us
    pallas_call x1, Pallas kernels, score(): pl.pallas_call(score_kernel, out_shape=(jax.ShapeDtypeStruct((2, rows.sha...  1.59 us
  transfers between devices with their start and end apart: 32, of which 12 were waited for; matrix products, arithmetic and copies ran while one was open for 2% of the time, Pallas kernels for 32%

profile of v1, /device:TPU:0, one launch (start us, length us, event | category | flops | bytes accessed | tf_op | source)
XLA Modules:
  0.0 72.6 jit_solution(12739722693405638857)
XLA Ops:
  1.9 2.5 %collective-permute-start.7 = (s32[1,32]{1,0:T(1,128)S(1)}, s32[1,32]{1,0:T(1,128)S(1)}, u32[]{:S(2)}, u32[]{:S(2)}) collective-permute-start(s32[1,32]{1,0:T(1,128)S(1)} %reshape.64), channel_id=1, source_target_pairs={{0,2},{1,3},{2,0},{3,1},{4,6},{5,7},{6,4},{7,5},{8,10},{9,11},{10,... | collective-permute-start | bytes 392 | tf_op jit(solution)/shard_map/ppermute | solution.py:45
  4.7 1.3 %collective-permute-done.7 = s32[1,32]{1,0:T(1,128)S(1)} collective-permute-done((s32[1,32]{1,0:T(1,128)S(1)}, s32[1,32]{1,0:T(1,128)S(1)}, u32[]{:S(2)}, u32[]{:S(2)}) %collective-permute-start.7) | collective-permute-done | bytes 160 | tf_op jit(solution)/shard_map/ppermute | solution.py:45
  6.0 2.0 %collective-permute-start.11 = (bf16[2,128,1024]{2,1,0:T(8,128)(2,1)}, bf16[2,128,1024]{2,1,0:T(8,128)(2,1)S(1)}, u32[]{:S(2)}, u32[]{:S(2)}) collective-permute-start(bf16[2,128,1024]{2,1,0:T(8,128)(2,1)} %states.1), channel_id=1, source_target_pairs={{0,2},{1,3},{2,0},{3,1},{4,6},{5,7},{6,4},{7,5},{8,10},{9,11},{10,... | collective-permute-start | bytes 1572872 | tf_op jit(solution)/shard_map/ppermute | solution.py:45
  8.1 1.5 %collective-permute-start.8 = (s32[1,64]{1,0:T(1,128)S(1)}, s32[1,64]{1,0:T(1,128)S(1)}, u32[]{:S(2)}, u32[]{:S(2)}) collective-permute-start(s32[1,64]{1,0:T(1,128)S(1)} %pad_add_fusion.3), channel_id=1, source_target_pairs={{0,4},{4,0},{8,12},{12,8},{16,20},{20,16},{24,28},{28,24},{1,5},{5... | collective-permute-start | bytes 776 | tf_op jit(solution)/shard_map/ppermute | solution.py:45
  9.6 2.0 %collective-permute-done.8 = s32[1,64]{1,0:T(1,128)S(1)} collective-permute-done((s32[1,64]{1,0:T(1,128)S(1)}, s32[1,64]{1,0:T(1,128)S(1)}, u32[]{:S(2)}, u32[]{:S(2)}) %collective-permute-start.8) | collective-permute-done | bytes 288 | tf_op jit(solution)/shard_map/ppermute | solution.py:45
  11.7 1.6 %collective-permute-start.9 = (s32[2,64]{1,0:T(2,128)S(1)}, s32[2,64]{1,0:T(2,128)S(1)}, u32[]{:S(2)}, u32[]{:S(2)}) collective-permute-start(s32[2,64]{1,0:T(2,128)S(1)} %pad_add_fusion.2), channel_id=1, source_target_pairs={{0,8},{4,12},{8,0},{12,4},{16,24},{20,28},{24,16},{28,20},{1,9},{5... | collective-permute-start | bytes 1544 | tf_op jit(solution)/shard_map/ppermute | solution.py:45
  13.3 2.0 %collective-permute-done.9 = s32[2,64]{1,0:T(2,128)S(1)} collective-permute-done((s32[2,64]{1,0:T(2,128)S(1)}, s32[2,64]{1,0:T(2,128)S(1)}, u32[]{:S(2)}, u32[]{:S(2)}) %collective-permute-start.9) | collective-permute-done | bytes 544 | tf_op jit(solution)/shard_map/ppermute | solution.py:45
  15.3 2.6 %collective-permute-start.10 = (s32[4,64]{1,0:T(4,128)S(1)}, s32[4,64]{1,0:T(4,128)S(1)}, u32[]{:S(2)}, u32[]{:S(2)}) collective-permute-start(s32[4,64]{1,0:T(4,128)S(1)} %pad_add_fusion.1), channel_id=1, source_target_pairs={{0,16},{4,20},{8,24},{12,28},{16,0},{20,4},{24,8},{28,12},{1,17},{... | collective-permute-start | bytes 3080 | tf_op jit(solution)/shard_map/ppermute | solution.py:45
  17.9 1.6 %load.1 = (bf16[128,1024]{1,0:T(8,128)(2,1)S(1)}, bf16[3,1024,256]{2,1,0:T(8,128)(2,1)S(1)}, bf16[128,1024]{1,0:T(8,128)(2,1)S(1)}) custom-call(bf16[2,128,1024]{2,1,0:T(8,128)(2,1)} %states.1, bf16[3,1024,256]{2,1,0:T(8,128)(2,1)} %bitcast.85, bf16[256,1024]{1,0:T(8,128)(2,1)} %w.1), custom_call_target="tpu_custom_call" | custom-call | flops 1 | bytes 1 | tf_op jit(solution)/shard_map/load/pallas_call | solution.py:80
  21.9 1.8 %collective-permute-done.17.i1 = s32[8,64]{1,0:T(8,128)S(1)} collective-permute-done((s32[8,64]{1,0:T(8,128)S(1)}, s32[8,64]{1,0:T(8,128)S(1)}, u32[]{:S(2)}, u32[]{:S(2)}) %collective-permute-start.17) | collective-permute-done | bytes 2080 | tf_op jit(solution)/shard_map/ppermute | solution.py:45
  24.8 3.7 %attention_own.1 = (bf16[512,256]{1,0:T(8,128)(2,1)S(1)}, bf16[512,1024]{1,0:T(8,128)(2,1)S(1)}) custom-call(s32[2]{0:T(128)} %lengths.7, bf16[128,1024]{1,0:T(8,128)(2,1)S(1)} %get-tuple-element.129.mine, bf16[2,128,1024]{2,1,0:T(8,128)(2,1)S(1)} %collective-permute-done.12.s1, bf16[2,128,1024]{2,1,0:T(8,128)(2,1)S(1)} %collective-permute-done.11.s2, ...), custom_call_target="tpu_custom_call" | custom-call | flops 1 | bytes 1 | tf_op jit(solution)/shard_map/attention_own/pallas_call | solution.py:165
  28.6 1.6 %collective-permute-start.19 = (bf16[512,256]{1,0:T(8,128)(2,1)S(1)}, bf16[512,256]{1,0:T(8,128)(2,1)S(1)}, u32[]{:S(2)}, u32[]{:S(2)}) collective-permute-start(bf16[512,256]{1,0:T(8,128)(2,1)S(1)} %get-tuple-element.136.here), channel_id=1, source_target_pairs={{0,2},{1,3},{2,0},{3,1},{4,6},{5,7},{6,4},{7,5},{8,10},{9,11},{10,... | collective-permute-start | bytes 786440 | tf_op jit(solution)/shard_map/ppermute | solution.py:45
  30.2 4.4 %attention_partner.1 = (bf16[512,256]{1,0:T(8,128)(2,1)S(1)}, s32[2,128]{1,0:T(2,128)S(1)}, bf16[128,128]{1,0:T(8,128)(2,1)S(1)}, s32[1]{0:T(128)}) custom-call(s32[2]{0:T(128)} %lengths.7, bf16[512,1024]{1,0:T(8,128)(2,1)S(1)} %get-tuple-element.138.text, bf16[3,1024,256]{2,1,0:T(8,128)(2,1)S(1)} %collective-permute-done.13.w, ...), custom_call_target="tpu_custom_call" | custom-call | flops 6000000000 | bytes 1048576 | tf_op jit(solution)/shard_map/attention_partner/pallas_call | solution.py:184
  34.6 1.6 %collective-permute-start.22 = (bf16[128,1024]{1,0:T(8,128)(2,1)S(1)}, bf16[128,1024]{1,0:T(8,128)(2,1)S(1)}, u32[]{:S(2)}, u32[]{:S(2)}) collective-permute-start(bf16[128,1024]{1,0:T(8,128)(2,1)S(1)} %collective-permute-done.21.half_0), channel_id=1, source_target_pairs={{0,4},{4,0},{8,12},{12,8},{16,20},{20,16},{24,28},{28,24},{1,5},{5... | collective-permute-start | bytes 786440 | tf_op jit(solution)/shard_map/ppermute | solution.py:45
  36.2 2.3 %collective-permute-done.19.there = bf16[512,256]{1,0:T(8,128)(2,1)S(1)} collective-permute-done((bf16[512,256]{1,0:T(8,128)(2,1)S(1)}, bf16[512,256]{1,0:T(8,128)(2,1)S(1)}, u32[]{:S(2)}, u32[]{:S(2)}) %collective-permute-start.19) | collective-permute-done | bytes 262176 | tf_op jit(solution)/shard_map/ppermute | solution.py:45
  39.0 3.7 %project_first.1 = (f32[512,1024]{1,0:T(8,128)S(1)}, bf16[64,1024]{1,0:T(8,128)(2,1)S(1)}, bf16[64,1024]{1,0:T(8,128)(2,1)S(1)}) custom-call(bf16[512,1024]{1,0:T(8,128)(2,1)S(1)} %get-tuple-element.138.text, bf16[512,256]{1,0:T(8,128)(2,1)S(1)} %get-tuple-element.136.here, bf16[256,1024]{1,0:T(8,128)(2,1)S(1)} %copy-done, f32[1,1024]{1,0:T(1,128)S(1)} %bitcast.69, ...), custom_call_target="tpu_custom_call" | custom-call | flops 1000000000 | bytes 1048576 | tf_op jit(solution)/shard_map/project_first/pallas_call | solution.py:224
  44.2 3.0 %collective-permute-start.31 = (bf16[1,4,16,1024]{3,2,0,1:T(8,128)(2,1)S(1)}, bf16[1,4,16,1024]{3,2,0,1:T(8,128)(2,1)S(1)}, u32[]{:S(2)}, u32[]{:S(2)}) collective-permute-start(bf16[1,4,16,1024]{3,2,0,1:T(8,128)(2,1)S(1)} %bitcast.70), channel_id=1, source_target_pairs={{0,16},{4,20},{8,24},{12,28},{16,0},{20,4},{24,8},{28,12},{1,17},{... | collective-permute-start | bytes 393224 | tf_op jit(solution)/shard_map/ppermute | solution.py:45
  47.3 3.8 %feed_there.1 = bf16[256,1024]{1,0:T(8,128)(2,1)S(1)} custom-call(f32[512,1024]{1,0:T(8,128)S(1)} %project_second.1.refs_0_, bf16[512,256]{1,0:T(8,128)(2,1)S(1)} %collective-permute-done.23.refs_1_, bf16[128,1024]{1,0:T(8,128)(2,1)S(1)} %collective-permute-done.24.refs_2_, bf16[128,1024]{1,0:T(8,128)(2,1)S(1)} %collective-permute-done.25.refs_3_, ...), custom_call_target="tpu_custom_call" | custom-call | flops 8000000000 | bytes 1048576 | tf_op jit(solution)/shard_map/feed_there/pallas_call | solution.py:295
  52.2 1.6 %collective-permute-done.31 = bf16[1,4,16,1024]{3,2,0,1:T(8,128)(2,1)S(1)} collective-permute-done((bf16[1,4,16,1024]{3,2,0,1:T(8,128)(2,1)S(1)}, bf16[1,4,16,1024]{3,2,0,1:T(8,128)(2,1)S(1)}, u32[]{:S(2)}, u32[]{:S(2)}) %collective-permute-start.31) | collective-permute-done | bytes 131104 | tf_op jit(solution)/shard_map/ppermute | solution.py:45
  53.8 1.4 %collective-permute-start.34 = (bf16[2,16,1024]{2,1,0:T(8,128)(2,1)S(1)}, bf16[2,16,1024]{2,1,0:T(8,128)(2,1)S(1)}, u32[]{:S(2)}, u32[]{:S(2)}) collective-permute-start(bf16[2,16,1024]{2,1,0:T(8,128)(2,1)S(1)} %get-tuple-element.191), channel_id=1, source_target_pairs={{0,12},{4,8},{8,4},{12,0},{16,28},{20,24},{24,20},{28,16},{1,13},{... | collective-permute-start | bytes 196616 | tf_op jit(solution)/shard_map/ppermute | solution.py:45
  55.7 1.7 %collective-permute-start.33 = (bf16[2,16,1024]{2,1,0:T(8,128)(2,1)S(1)}, bf16[2,16,1024]{2,1,0:T(8,128)(2,1)S(1)}, u32[]{:S(2)}, u32[]{:S(2)}) collective-permute-start(bf16[2,16,1024]{2,1,0:T(8,128)(2,1)S(1)} %get-tuple-element.194), channel_id=1, source_target_pairs={{0,8},{4,12},{8,0},{12,4},{16,24},{20,28},{24,16},{28,20},{1,9},{5... | collective-permute-start | bytes 196616 | tf_op jit(solution)/shard_map/ppermute | solution.py:45
  57.4 3.8 %feed_here.1.here = f32[256,1024]{1,0:T(8,128)S(1)} custom-call(f32[512,1024]{1,0:T(8,128)S(1)} %project_second.1.refs_0_, bf16[512,256]{1,0:T(8,128)(2,1)S(1)} %collective-permute-done.23.refs_1_, bf16[128,1024]{1,0:T(8,128)(2,1)S(1)} %collective-permute-done.24.refs_2_, bf16[128,1024]{1,0:T(8,128)(2,1)S(1)} %collective-permute-done.25.refs_3_, ...), custom_call_target="tpu_custom_call" | custom-call | flops 8000000000 | bytes 1048576 | tf_op jit(solution)/shard_map/feed_here/pallas_call | solution.py:295
  63.7 1.8 %collective-permute-done.27.there = bf16[256,1024]{1,0:T(8,128)(2,1)S(1)} collective-permute-done((bf16[256,1024]{1,0:T(8,128)(2,1)S(1)}, bf16[256,1024]{1,0:T(8,128)(2,1)S(1)}, u32[]{:S(2)}, u32[]{:S(2)}) %collective-permute-start.27) | collective-permute-done | bytes 524320 | tf_op jit(solution)/shard_map/ppermute | solution.py:45
  71.0 1.6 %score.1 = (f32[2,16]{1,0:T(2,128)}, bf16[2,128,1024]{2,1,0:T(8,128)(2,1)}) custom-call(s32[2]{0:T(128)S(1)} %copy-done.2, f32[1,1024]{1,0:T(1,128)S(1)} %get-tuple-element.155.pool, f32[1,1024]{1,0:T(1,128)S(1)} %collective-permute-done.28.pool_core, f32[1,1024]{1,0:T(1,128)S(1)} %collective-permute-done.29.pool_chip, ...), custom_call_target="tpu_custom_call" | custom-call | flops 1000000000 | bytes 1048576 | tf_op jit(solution)/shard_map/score/pallas_call | solution.py:367
  (81 shorter events, 16.6 us)
Async XLA Ops:
  0.7 20.3 %collective-permute-start.13 = (bf16[3,1024,256]{2,1,0:T(8,128)(2,1)}, bf16[3,1024,256]{2,1,0:T(8,128)(2,1)S(1)}, u32[]{:S(2)}, u32[]{:S(2)}) collective-permute-start(bf16[3,1024,256]{2,1,0:T(8,128)(2,1)} %bitcast.84), channel_id=1, source_target_pairs={{0,1},{1,0},{2,3},{3,2},{4,5},{5,4},{6,7},{7,6},{8,9},{9,8},{10,11... | collective-permute-start | bytes 4718600 | tf_op jit(solution)/shard_map/ppermute | solution.py:45
  1.9 4.0 %collective-permute-start.7 = (s32[1,32]{1,0:T(1,128)S(1)}, s32[1,32]{1,0:T(1,128)S(1)}, u32[]{:S(2)}, u32[]{:S(2)}) collective-permute-start(s32[1,32]{1,0:T(1,128)S(1)} %reshape.64), channel_id=1, source_target_pairs={{0,2},{1,3},{2,0},{3,1},{4,6},{5,7},{6,4},{7,5},{8,10},{9,11},{10,... | collective-permute-start | bytes 392 | tf_op jit(solution)/shard_map/ppermute | solution.py:45
  4.4 16.5 %collective-permute-start.12 = (bf16[2,128,1024]{2,1,0:T(8,128)(2,1)}, bf16[2,128,1024]{2,1,0:T(8,128)(2,1)S(1)}, u32[]{:S(2)}, u32[]{:S(2)}) collective-permute-start(bf16[2,128,1024]{2,1,0:T(8,128)(2,1)} %states.1), channel_id=1, source_target_pairs={{0,1},{1,0},{2,3},{3,2},{4,5},{5,4},{6,7},{7,6},{8,9},{9,8},{10,11... | collective-permute-start | bytes 1572872 | tf_op jit(solution)/shard_map/ppermute | solution.py:45
  6.0 14.9 %collective-permute-start.11 = (bf16[2,128,1024]{2,1,0:T(8,128)(2,1)}, bf16[2,128,1024]{2,1,0:T(8,128)(2,1)S(1)}, u32[]{:S(2)}, u32[]{:S(2)}) collective-permute-start(bf16[2,128,1024]{2,1,0:T(8,128)(2,1)} %states.1), channel_id=1, source_target_pairs={{0,2},{1,3},{2,0},{3,1},{4,6},{5,7},{6,4},{7,5},{8,10},{9,11},{10,... | collective-permute-start | bytes 1572872 | tf_op jit(solution)/shard_map/ppermute | solution.py:45
  8.1 3.5 %collective-permute-start.8 = (s32[1,64]{1,0:T(1,128)S(1)}, s32[1,64]{1,0:T(1,128)S(1)}, u32[]{:S(2)}, u32[]{:S(2)}) collective-permute-start(s32[1,64]{1,0:T(1,128)S(1)} %pad_add_fusion.3), channel_id=1, source_target_pairs={{0,4},{4,0},{8,12},{12,8},{16,20},{20,16},{24,28},{28,24},{1,5},{5... | collective-permute-start | bytes 776 | tf_op jit(solution)/shard_map/ppermute | solution.py:45
  11.7 3.6 %collective-permute-start.9 = (s32[2,64]{1,0:T(2,128)S(1)}, s32[2,64]{1,0:T(2,128)S(1)}, u32[]{:S(2)}, u32[]{:S(2)}) collective-permute-start(s32[2,64]{1,0:T(2,128)S(1)} %pad_add_fusion.2), channel_id=1, source_target_pairs={{0,8},{4,12},{8,0},{12,4},{16,24},{20,28},{24,16},{28,20},{1,9},{5... | collective-permute-start | bytes 1544 | tf_op jit(solution)/shard_map/ppermute | solution.py:45
  15.3 4.5 %collective-permute-start.10 = (s32[4,64]{1,0:T(4,128)S(1)}, s32[4,64]{1,0:T(4,128)S(1)}, u32[]{:S(2)}, u32[]{:S(2)}) collective-permute-start(s32[4,64]{1,0:T(4,128)S(1)} %pad_add_fusion.1), channel_id=1, source_target_pairs={{0,16},{4,20},{8,24},{12,28},{16,0},{20,4},{24,8},{28,12},{1,17},{... | collective-permute-start | bytes 3080 | tf_op jit(solution)/shard_map/ppermute | solution.py:45
  23.7 6.4 %collective-permute-start.20 = (bf16[1024,1024]{1,0:T(8,128)(2,1)S(1)}, bf16[1024,1024]{1,0:T(8,128)(2,1)S(1)}, u32[]{:S(2)}, u32[]{:S(2)}) collective-permute-start(bf16[1024,1024]{1,0:T(8,128)(2,1)S(1)} %copy-done.10), channel_id=1, source_target_pairs={{0,1},{1,0},{2,3},{3,2},{4,5},{5,4},{6,7},{7,6},{8,9},{9,8},{10,11... | collective-permute-start | bytes 6291464 | tf_op jit(solution)/shard_map/ppermute | solution.py:45
  24.1 23.1 %collective-permute-start.26 = (bf16[1024,1024]{1,0:T(8,128)(2,1)}, bf16[1024,1024]{1,0:T(8,128)(2,1)S(1)}, u32[]{:S(2)}, u32[]{:S(2)}) collective-permute-start(bf16[1024,1024]{1,0:T(8,128)(2,1)} %refs_11_.3), channel_id=1, source_target_pairs={{0,1},{1,0},{2,3},{3,2},{4,5},{5,4},{6,7},{7,6},{8,9},{9,8},{10,11... | collective-permute-start | bytes 6291464 | tf_op jit(solution)/shard_map/ppermute | solution.py:45
  24.3 10.2 %collective-permute-start.21 = (bf16[128,1024]{1,0:T(8,128)(2,1)S(1)}, bf16[128,1024]{1,0:T(8,128)(2,1)S(1)}, u32[]{:S(2)}, u32[]{:S(2)}) collective-permute-start(bf16[128,1024]{1,0:T(8,128)(2,1)S(1)} %get-tuple-element.147), channel_id=1, source_target_pairs={{0,2},{1,3},{2,0},{3,1},{4,6},{5,7},{6,4},{7,5},{8,10},{9,11},{10,... | collective-permute-start | bytes 786440 | tf_op jit(solution)/shard_map/ppermute | solution.py:45
  28.6 9.9 %collective-permute-start.19 = (bf16[512,256]{1,0:T(8,128)(2,1)S(1)}, bf16[512,256]{1,0:T(8,128)(2,1)S(1)}, u32[]{:S(2)}, u32[]{:S(2)}) collective-permute-start(bf16[512,256]{1,0:T(8,128)(2,1)S(1)} %get-tuple-element.136.here), channel_id=1, source_target_pairs={{0,2},{1,3},{2,0},{3,1},{4,6},{5,7},{6,4},{7,5},{8,10},{9,11},{10,... | collective-permute-start | bytes 786440 | tf_op jit(solution)/shard_map/ppermute | solution.py:45
  34.6 8.3 %collective-permute-start.22 = (bf16[128,1024]{1,0:T(8,128)(2,1)S(1)}, bf16[128,1024]{1,0:T(8,128)(2,1)S(1)}, u32[]{:S(2)}, u32[]{:S(2)}) collective-permute-start(bf16[128,1024]{1,0:T(8,128)(2,1)S(1)} %collective-permute-done.21.half_0), channel_id=1, source_target_pairs={{0,4},{4,0},{8,12},{12,8},{16,20},{20,16},{24,28},{28,24},{1,5},{5... | collective-permute-start | bytes 786440 | tf_op jit(solution)/shard_map/ppermute | solution.py:45
  38.5 8.8 %collective-permute-start.23 = (bf16[512,256]{1,0:T(8,128)(2,1)S(1)}, bf16[512,256]{1,0:T(8,128)(2,1)S(1)}, u32[]{:S(2)}, u32[]{:S(2)}) collective-permute-start(bf16[512,256]{1,0:T(8,128)(2,1)S(1)} %get-tuple-element.145.context), channel_id=1, source_target_pairs={{0,2},{1,3},{2,0},{3,1},{4,6},{5,7},{6,4},{7,5},{8,10},{9,11},{10,... | collective-permute-start | bytes 786440 | tf_op jit(solution)/shard_map/ppermute | solution.py:45
  42.8 4.5 %collective-permute-start.24 = (bf16[128,1024]{1,0:T(8,128)(2,1)S(1)}, bf16[128,1024]{1,0:T(8,128)(2,1)S(1)}, u32[]{:S(2)}, u32[]{:S(2)}) collective-permute-start(bf16[128,1024]{1,0:T(8,128)(2,1)S(1)} %collective-permute-done.21.half_0), channel_id=1, source_target_pairs={{0,1},{1,0},{2,3},{3,2},{4,5},{5,4},{6,7},{7,6},{8,9},{9,8},{10,11... | collective-permute-start | bytes 786440 | tf_op jit(solution)/shard_map/ppermute | solution.py:45
  42.9 4.4 %collective-permute-start.25 = (bf16[128,1024]{1,0:T(8,128)(2,1)S(1)}, bf16[128,1024]{1,0:T(8,128)(2,1)S(1)}, u32[]{:S(2)}, u32[]{:S(2)}) collective-permute-start(bf16[128,1024]{1,0:T(8,128)(2,1)S(1)} %collective-permute-done.22.half_1), channel_id=1, source_target_pairs={{0,1},{1,0},{2,3},{3,2},{4,5},{5,4},{6,7},{7,6},{8,9},{9,8},{10,11... | collective-permute-start | bytes 786440 | tf_op jit(solution)/shard_map/ppermute | solution.py:45
  44.2 9.6 %collective-permute-start.31 = (bf16[1,4,16,1024]{3,2,0,1:T(8,128)(2,1)S(1)}, bf16[1,4,16,1024]{3,2,0,1:T(8,128)(2,1)S(1)}, u32[]{:S(2)}, u32[]{:S(2)}) collective-permute-start(bf16[1,4,16,1024]{3,2,0,1:T(8,128)(2,1)S(1)} %bitcast.70), channel_id=1, source_target_pairs={{0,16},{4,20},{8,24},{12,28},{16,0},{20,4},{24,8},{28,12},{1,17},{... | collective-permute-start | bytes 393224 | tf_op jit(solution)/shard_map/ppermute | solution.py:45
  51.1 14.4 %collective-permute-start.27 = (bf16[256,1024]{1,0:T(8,128)(2,1)S(1)}, bf16[256,1024]{1,0:T(8,128)(2,1)S(1)}, u32[]{:S(2)}, u32[]{:S(2)}) collective-permute-start(bf16[256,1024]{1,0:T(8,128)(2,1)S(1)} %feed_there.1), channel_id=1, source_target_pairs={{0,2},{1,3},{2,0},{3,1},{4,6},{5,7},{6,4},{7,5},{8,10},{9,11},{10,... | collective-permute-start | bytes 1572872 | tf_op jit(solution)/shard_map/ppermute | solution.py:45
  53.8 7.4 %collective-permute-start.34 = (bf16[2,16,1024]{2,1,0:T(8,128)(2,1)S(1)}, bf16[2,16,1024]{2,1,0:T(8,128)(2,1)S(1)}, u32[]{:S(2)}, u32[]{:S(2)}) collective-permute-start(bf16[2,16,1024]{2,1,0:T(8,128)(2,1)S(1)} %get-tuple-element.191), channel_id=1, source_target_pairs={{0,12},{4,8},{8,4},{12,0},{16,28},{20,24},{24,20},{28,16},{1,13},{... | collective-permute-start | bytes 196616 | tf_op jit(solution)/shard_map/ppermute | solution.py:45
  55.2 6.0 %collective-permute-start.32 = (bf16[2,16,1024]{2,1,0:T(8,128)(2,1)S(1)}, bf16[2,16,1024]{2,1,0:T(8,128)(2,1)S(1)}, u32[]{:S(2)}, u32[]{:S(2)}) collective-permute-start(bf16[2,16,1024]{2,1,0:T(8,128)(2,1)S(1)} %get-tuple-element.193), channel_id=1, source_target_pairs={{0,4},{4,0},{8,12},{12,8},{16,20},{20,16},{24,28},{28,24},{1,5},{5... | collective-permute-start | bytes 196616 | tf_op jit(solution)/shard_map/ppermute | solution.py:45
  55.7 5.6 %collective-permute-start.33 = (bf16[2,16,1024]{2,1,0:T(8,128)(2,1)S(1)}, bf16[2,16,1024]{2,1,0:T(8,128)(2,1)S(1)}, u32[]{:S(2)}, u32[]{:S(2)}) collective-permute-start(bf16[2,16,1024]{2,1,0:T(8,128)(2,1)S(1)} %get-tuple-element.194), channel_id=1, source_target_pairs={{0,8},{4,12},{8,0},{12,4},{16,24},{20,28},{24,16},{28,20},{1,9},{5... | collective-permute-start | bytes 196616 | tf_op jit(solution)/shard_map/ppermute | solution.py:45
  61.5 6.3 %collective-permute-start.35 = (bf16[32,1024]{1,0:T(8,128)(2,1)S(1)}, bf16[32,1024]{1,0:T(8,128)(2,1)S(1)}, u32[]{:S(2)}, u32[]{:S(2)}) collective-permute-start(bf16[32,1024]{1,0:T(8,128)(2,1)S(1)} %get-tuple-element.188), channel_id=1, source_target_pairs={{0,2},{1,3},{2,0},{3,1},{4,6},{5,7},{6,4},{7,5},{8,10},{9,11},{10,... | collective-permute-start | bytes 196616 | tf_op jit(solution)/shard_map/ppermute | solution.py:45
  62.7 5.8 %collective-permute-start.37 = (bf16[32,1024]{1,0:T(8,128)(2,1)S(1)}, bf16[32,1024]{1,0:T(8,128)(2,1)S(1)}, u32[]{:S(2)}, u32[]{:S(2)}) collective-permute-start(bf16[32,1024]{1,0:T(8,128)(2,1)S(1)} %get-tuple-element.189), channel_id=1, source_target_pairs={{0,3},{1,2},{2,1},{3,0},{4,7},{5,6},{6,5},{7,4},{8,11},{9,10},{10,... | collective-permute-start | bytes 196616 | tf_op jit(solution)/shard_map/ppermute | solution.py:45
  62.7 5.8 %collective-permute-start.36 = (bf16[32,1024]{1,0:T(8,128)(2,1)S(1)}, bf16[32,1024]{1,0:T(8,128)(2,1)S(1)}, u32[]{:S(2)}, u32[]{:S(2)}) collective-permute-start(bf16[32,1024]{1,0:T(8,128)(2,1)S(1)} %get-tuple-element.190), channel_id=1, source_target_pairs={{0,1},{1,0},{2,3},{3,2},{4,5},{5,4},{6,7},{7,6},{8,9},{9,8},{10,11... | collective-permute-start | bytes 196616 | tf_op jit(solution)/shard_map/ppermute | solution.py:45
  66.7 3.7 %collective-permute-start.29 = (f32[1,1024]{1,0:T(1,128)S(1)}, f32[1,1024]{1,0:T(1,128)S(1)}, u32[]{:S(2)}, u32[]{:S(2)}) collective-permute-start(f32[1,1024]{1,0:T(1,128)S(1)} %get-tuple-element.155.pool), channel_id=1, source_target_pairs={{0,2},{1,3},{2,0},{3,1},{4,6},{5,7},{6,4},{7,5},{8,10},{9,11},{10,... | collective-permute-start | bytes 12296 | tf_op jit(solution)/shard_map/ppermute | solution.py:45
  (19 other events, 149.9 us)

commit v2 on v1

--- a/solution.py
+++ b/solution.py
@@ -134,8 +134,8 @@
         lanes = slice(pair * 128, (pair + 1) * 128)
         k_pair = parts[1, :, lanes]
         v_ones = jnp.concatenate([parts[2, :, lanes], ones], axis=1)
-        for block in range(4):
-            rows = slice(block * share, (block + 1) * share)
+        for block in range(2):
+            rows = slice(2 * block * share, 2 * (block + 1) * share)
             q_pair = parts[0, rows, lanes] * scale
             zero = jnp.zeros((), BF16)
             q_heads = jnp.concatenate(
@@ -150,7 +150,7 @@
             expo = jnp.exp(logits - top).astype(BF16)
             summed = matmul(expo, v_ones)
             found = summed[:, :128] / summed[:, 128:]
-            context = jnp.where(low, found[:share], found[share:])
+            context = jnp.where(low, found[: 2 * share], found[2 * share :])
             context = jnp.where(row_pos[rows] < length, context, F32(0.0))
             out[rows, lanes] = context.astype(BF16)
 
@@ -616,8 +616,9 @@
     b_qkv_p = swap(b_qkv, "tp", 1)
     b_up_p = swap(b_up, "tp", 1)
 
-    held = cand_ids.reshape(1, -1)
-    held = jnp.concatenate([held, swap(held, "tp", 2)], axis=1)
+    held = jnp.concatenate(
+        [cand_ids.reshape(1, -1), swap(cand_ids, "tp", 2).reshape(1, -1)], axis=1
+    )
     from_chip = swap(after(states, held), "tp", 2)
     for mask in masks("req"):
         other = swap(held, "req", mask)

time: 72.9 us -> 72.4 us (level)
  no operation moved by 1% of the time
where the time goes in v2:
time: 72.4 us; the launch traced here: 72 us
  starting transfers between devices  28.9 us (40%)
  Pallas kernels  24.7 us (34%)
  waiting for transfers between devices  15.5 us (21%)
  between operations  0.94 us (1%)
  local copies, waits for them, and re-layouts  0.91 us (1%)
    ppermute x32, starting transfers between devices, swap(): return lax.ppermute(value, axis, [(i, i ^ mask) for i in range(count)])  28.9 us
    ppermute x32, waiting for transfers between devices, swap(): return lax.ppermute(value, axis, [(i, i ^ mask) for i in range(count)])  15.5 us
    pallas_call x2, Pallas kernels, feed_forward(): pl.pallas_call(lambda *refs: feed_kernel(keep_rest, *refs), out_shape=jax...  7.62 us
    pallas_call x1, Pallas kernels, project_first(): pl.pallas_call(project_first_kernel, out_shape=(jax.ShapeDtypeStruct((seq...  4.21 us
    pallas_call x1, Pallas kernels, second_attention(): pl.pallas_call(functools.partial(second_attention_kernel, rows_here), out...  4.11 us
    pallas_call x1, Pallas kernels, first_attention(): pl.pallas_call(first_attention_kernel, out_shape=(jax.ShapeDtypeStruct((4...  3.44 us
    pallas_call x1, Pallas kernels, load(): pl.pallas_call(load_kernel, out_shape=(jax.ShapeDtypeStruct(states.shape[...  1.61 us
    pallas_call x1, Pallas kernels, score(): pl.pallas_call(score_kernel, out_shape=(jax.ShapeDtypeStruct((2, rows.sha...  1.59 us
  transfers between devices with their start and end apart: 32, of which 12 were waited for; matrix products, arithmetic and copies ran while one was open for 2% of the time, Pallas kernels for 32%

profile of v2, /device:TPU:0, one launch (start us, length us, event | category | flops | bytes accessed | tf_op | source)
XLA Modules:
  0.0 72.0 jit_solution(14283142982962690980)
XLA Ops:
  1.2 2.6 %collective-permute-start.7 = (s32[2,16]{1,0:T(2,128)}, s32[2,16]{1,0:T(2,128)S(1)}, u32[]{:S(2)}, u32[]{:S(2)}) collective-permute-start(s32[2,16]{1,0:T(2,128)} %param.33), channel_id=1, source_target_pairs={{0,2},{1,3},{2,0},{3,1},{4,6},{5,7},{6,4},{7,5},{8,10},{9,11},{10,... | collective-permute-start | bytes 392 | tf_op jit(solution)/shard_map/ppermute | solution.py:45
  5.7 2.0 %collective-permute-start.11 = (bf16[2,128,1024]{2,1,0:T(8,128)(2,1)}, bf16[2,128,1024]{2,1,0:T(8,128)(2,1)S(1)}, u32[]{:S(2)}, u32[]{:S(2)}) collective-permute-start(bf16[2,128,1024]{2,1,0:T(8,128)(2,1)} %states.1), channel_id=1, source_target_pairs={{0,2},{1,3},{2,0},{3,1},{4,6},{5,7},{6,4},{7,5},{8,10},{9,11},{10,... | collective-permute-start | bytes 1572872 | tf_op jit(solution)/shard_map/ppermute | solution.py:45
  7.7 1.5 %collective-permute-start.8 = (s32[1,64]{1,0:T(1,128)S(1)}, s32[1,64]{1,0:T(1,128)S(1)}, u32[]{:S(2)}, u32[]{:S(2)}) collective-permute-start(s32[1,64]{1,0:T(1,128)S(1)} %pad_add_fusion.3), channel_id=1, source_target_pairs={{0,4},{4,0},{8,12},{12,8},{16,20},{20,16},{24,28},{28,24},{1,5},{5... | collective-permute-start | bytes 776 | tf_op jit(solution)/shard_map/ppermute | solution.py:45
  9.2 2.0 %collective-permute-done.8 = s32[1,64]{1,0:T(1,128)S(1)} collective-permute-done((s32[1,64]{1,0:T(1,128)S(1)}, s32[1,64]{1,0:T(1,128)S(1)}, u32[]{:S(2)}, u32[]{:S(2)}) %collective-permute-start.8) | collective-permute-done | bytes 288 | tf_op jit(solution)/shard_map/ppermute | solution.py:45
  11.3 1.6 %collective-permute-start.9 = (s32[2,64]{1,0:T(2,128)S(1)}, s32[2,64]{1,0:T(2,128)S(1)}, u32[]{:S(2)}, u32[]{:S(2)}) collective-permute-start(s32[2,64]{1,0:T(2,128)S(1)} %pad_add_fusion.2), channel_id=1, source_target_pairs={{0,8},{4,12},{8,0},{12,4},{16,24},{20,28},{24,16},{28,20},{1,9},{5... | collective-permute-start | bytes 1544 | tf_op jit(solution)/shard_map/ppermute | solution.py:45
  12.9 2.0 %collective-permute-done.9 = s32[2,64]{1,0:T(2,128)S(1)} collective-permute-done((s32[2,64]{1,0:T(2,128)S(1)}, s32[2,64]{1,0:T(2,128)S(1)}, u32[]{:S(2)}, u32[]{:S(2)}) %collective-permute-start.9) | collective-permute-done | bytes 544 | tf_op jit(solution)/shard_map/ppermute | solution.py:45
  15.0 2.6 %collective-permute-start.10 = (s32[4,64]{1,0:T(4,128)S(1)}, s32[4,64]{1,0:T(4,128)S(1)}, u32[]{:S(2)}, u32[]{:S(2)}) collective-permute-start(s32[4,64]{1,0:T(4,128)S(1)} %pad_add_fusion.1), channel_id=1, source_target_pairs={{0,16},{4,20},{8,24},{12,28},{16,0},{20,4},{24,8},{28,12},{1,17},{... | collective-permute-start | bytes 3080 | tf_op jit(solution)/shard_map/ppermute | solution.py:45
  17.5 1.6 %load.1 = (bf16[128,1024]{1,0:T(8,128)(2,1)S(1)}, bf16[3,1024,256]{2,1,0:T(8,128)(2,1)S(1)}, bf16[128,1024]{1,0:T(8,128)(2,1)S(1)}) custom-call(bf16[2,128,1024]{2,1,0:T(8,128)(2,1)} %states.1, bf16[3,1024,256]{2,1,0:T(8,128)(2,1)} %bitcast.85, bf16[256,1024]{1,0:T(8,128)(2,1)} %w.1), custom_call_target="tpu_custom_call" | custom-call | flops 1 | bytes 1 | tf_op jit(solution)/shard_map/load/pallas_call | solution.py:80
  21.5 1.8 %collective-permute-done.17.i1 = s32[8,64]{1,0:T(8,128)S(1)} collective-permute-done((s32[8,64]{1,0:T(8,128)S(1)}, s32[8,64]{1,0:T(8,128)S(1)}, u32[]{:S(2)}, u32[]{:S(2)}) %collective-permute-start.17) | collective-permute-done | bytes 2080 | tf_op jit(solution)/shard_map/ppermute | solution.py:45
  24.5 3.4 %attention_own.1 = (bf16[512,256]{1,0:T(8,128)(2,1)S(1)}, bf16[512,1024]{1,0:T(8,128)(2,1)S(1)}) custom-call(s32[2]{0:T(128)} %lengths.7, bf16[128,1024]{1,0:T(8,128)(2,1)S(1)} %get-tuple-element.129.mine, bf16[2,128,1024]{2,1,0:T(8,128)(2,1)S(1)} %collective-permute-done.12.s1, bf16[2,128,1024]{2,1,0:T(8,128)(2,1)S(1)} %collective-permute-done.11.s2, ...), custom_call_target="tpu_custom_call" | custom-call | flops 1 | bytes 1 | tf_op jit(solution)/shard_map/attention_own/pallas_call | solution.py:165
  27.9 1.6 %collective-permute-start.19 = (bf16[512,256]{1,0:T(8,128)(2,1)S(1)}, bf16[512,256]{1,0:T(8,128)(2,1)S(1)}, u32[]{:S(2)}, u32[]{:S(2)}) collective-permute-start(bf16[512,256]{1,0:T(8,128)(2,1)S(1)} %get-tuple-element.136.here), channel_id=1, source_target_pairs={{0,2},{1,3},{2,0},{3,1},{4,6},{5,7},{6,4},{7,5},{8,10},{9,11},{10,... | collective-permute-start | bytes 786440 | tf_op jit(solution)/shard_map/ppermute | solution.py:45
  29.5 4.1 %attention_partner.1 = (bf16[512,256]{1,0:T(8,128)(2,1)S(1)}, s32[2,128]{1,0:T(2,128)S(1)}, bf16[128,128]{1,0:T(8,128)(2,1)S(1)}, s32[1]{0:T(128)}) custom-call(s32[2]{0:T(128)} %lengths.7, bf16[512,1024]{1,0:T(8,128)(2,1)S(1)} %get-tuple-element.138.text, bf16[3,1024,256]{2,1,0:T(8,128)(2,1)S(1)} %collective-permute-done.13.w, ...), custom_call_target="tpu_custom_call" | custom-call | flops 6000000000 | bytes 1048576 | tf_op jit(solution)/shard_map/attention_partner/pallas_call | solution.py:184
  33.6 1.6 %collective-permute-start.22 = (bf16[128,1024]{1,0:T(8,128)(2,1)S(1)}, bf16[128,1024]{1,0:T(8,128)(2,1)S(1)}, u32[]{:S(2)}, u32[]{:S(2)}) collective-permute-start(bf16[128,1024]{1,0:T(8,128)(2,1)S(1)} %collective-permute-done.21.half_0), channel_id=1, source_target_pairs={{0,4},{4,0},{8,12},{12,8},{16,20},{20,16},{24,28},{28,24},{1,5},{5... | collective-permute-start | bytes 786440 | tf_op jit(solution)/shard_map/ppermute | solution.py:45
  35.2 2.9 %collective-permute-done.19.there = bf16[512,256]{1,0:T(8,128)(2,1)S(1)} collective-permute-done((bf16[512,256]{1,0:T(8,128)(2,1)S(1)}, bf16[512,256]{1,0:T(8,128)(2,1)S(1)}, u32[]{:S(2)}, u32[]{:S(2)}) %collective-permute-start.19) | collective-permute-done | bytes 262176 | tf_op jit(solution)/shard_map/ppermute | solution.py:45
  38.6 4.2 %project_first.1 = (f32[512,1024]{1,0:T(8,128)S(1)}, bf16[64,1024]{1,0:T(8,128)(2,1)S(1)}, bf16[64,1024]{1,0:T(8,128)(2,1)S(1)}) custom-call(bf16[512,1024]{1,0:T(8,128)(2,1)S(1)} %get-tuple-element.138.text, bf16[512,256]{1,0:T(8,128)(2,1)S(1)} %get-tuple-element.136.here, bf16[256,1024]{1,0:T(8,128)(2,1)S(1)} %copy-done, f32[1,1024]{1,0:T(1,128)S(1)} %bitcast.69, ...), custom_call_target="tpu_custom_call" | custom-call | flops 1000000000 | bytes 1048576 | tf_op jit(solution)/shard_map/project_first/pallas_call | solution.py:224
  44.3 2.3 %collective-permute-start.31 = (bf16[1,4,16,1024]{3,2,0,1:T(8,128)(2,1)S(1)}, bf16[1,4,16,1024]{3,2,0,1:T(8,128)(2,1)S(1)}, u32[]{:S(2)}, u32[]{:S(2)}) collective-permute-start(bf16[1,4,16,1024]{3,2,0,1:T(8,128)(2,1)S(1)} %bitcast.70), channel_id=1, source_target_pairs={{0,16},{4,20},{8,24},{12,28},{16,0},{20,4},{24,8},{28,12},{1,17},{... | collective-permute-start | bytes 393224 | tf_op jit(solution)/shard_map/ppermute | solution.py:45
  46.7 3.8 %feed_there.1 = bf16[256,1024]{1,0:T(8,128)(2,1)S(1)} custom-call(f32[512,1024]{1,0:T(8,128)S(1)} %project_second.1.refs_0_, bf16[512,256]{1,0:T(8,128)(2,1)S(1)} %collective-permute-done.23.refs_1_, bf16[128,1024]{1,0:T(8,128)(2,1)S(1)} %collective-permute-done.24.refs_2_, bf16[128,1024]{1,0:T(8,128)(2,1)S(1)} %collective-permute-done.25.refs_3_, ...), custom_call_target="tpu_custom_call" | custom-call | flops 8000000000 | bytes 1048576 | tf_op jit(solution)/shard_map/feed_there/pallas_call | solution.py:295
  50.5 1.3 %collective-permute-start.27 = (bf16[256,1024]{1,0:T(8,128)(2,1)S(1)}, bf16[256,1024]{1,0:T(8,128)(2,1)S(1)}, u32[]{:S(2)}, u32[]{:S(2)}) collective-permute-start(bf16[256,1024]{1,0:T(8,128)(2,1)S(1)} %feed_there.1), channel_id=1, source_target_pairs={{0,2},{1,3},{2,0},{3,1},{4,6},{5,7},{6,4},{7,5},{8,10},{9,11},{10,... | collective-permute-start | bytes 1572872 | tf_op jit(solution)/shard_map/ppermute | solution.py:45
  51.8 1.8 %collective-permute-done.31 = bf16[1,4,16,1024]{3,2,0,1:T(8,128)(2,1)S(1)} collective-permute-done((bf16[1,4,16,1024]{3,2,0,1:T(8,128)(2,1)S(1)}, bf16[1,4,16,1024]{3,2,0,1:T(8,128)(2,1)S(1)}, u32[]{:S(2)}, u32[]{:S(2)}) %collective-permute-start.31) | collective-permute-done | bytes 131104 | tf_op jit(solution)/shard_map/ppermute | solution.py:45
  55.4 1.7 %collective-permute-start.33 = (bf16[2,16,1024]{2,1,0:T(8,128)(2,1)S(1)}, bf16[2,16,1024]{2,1,0:T(8,128)(2,1)S(1)}, u32[]{:S(2)}, u32[]{:S(2)}) collective-permute-start(bf16[2,16,1024]{2,1,0:T(8,128)(2,1)S(1)} %get-tuple-element.194), channel_id=1, source_target_pairs={{0,8},{4,12},{8,0},{12,4},{16,24},{20,28},{24,16},{28,20},{1,9},{5... | collective-permute-start | bytes 196616 | tf_op jit(solution)/shard_map/ppermute | solution.py:45
  57.1 3.8 %feed_here.1.here = f32[256,1024]{1,0:T(8,128)S(1)} custom-call(f32[512,1024]{1,0:T(8,128)S(1)} %project_second.1.refs_0_, bf16[512,256]{1,0:T(8,128)(2,1)S(1)} %collective-permute-done.23.refs_1_, bf16[128,1024]{1,0:T(8,128)(2,1)S(1)} %collective-permute-done.24.refs_2_, bf16[128,1024]{1,0:T(8,128)(2,1)S(1)} %collective-permute-done.25.refs_3_, ...), custom_call_target="tpu_custom_call" | custom-call | flops 8000000000 | bytes 1048576 | tf_op jit(solution)/shard_map/feed_here/pallas_call | solution.py:295
  63.5 1.4 %collective-permute-done.27.there = bf16[256,1024]{1,0:T(8,128)(2,1)S(1)} collective-permute-done((bf16[256,1024]{1,0:T(8,128)(2,1)S(1)}, bf16[256,1024]{1,0:T(8,128)(2,1)S(1)}, u32[]{:S(2)}, u32[]{:S(2)}) %collective-permute-start.27) | collective-permute-done | bytes 524320 | tf_op jit(solution)/shard_map/ppermute | solution.py:45
  66.1 1.3 %collective-permute-start.29 = (f32[1,1024]{1,0:T(1,128)S(1)}, f32[1,1024]{1,0:T(1,128)S(1)}, u32[]{:S(2)}, u32[]{:S(2)}) collective-permute-start(f32[1,1024]{1,0:T(1,128)S(1)} %get-tuple-element.155.pool), channel_id=1, source_target_pairs={{0,2},{1,3},{2,0},{3,1},{4,6},{5,7},{6,4},{7,5},{8,10},{9,11},{10,... | collective-permute-start | bytes 12296 | tf_op jit(solution)/shard_map/ppermute | solution.py:45
  70.4 1.6 %score.1 = (f32[2,16]{1,0:T(2,128)}, bf16[2,128,1024]{2,1,0:T(8,128)(2,1)}) custom-call(s32[2]{0:T(128)S(1)} %copy-done.2, f32[1,1024]{1,0:T(1,128)S(1)} %get-tuple-element.155.pool, f32[1,1024]{1,0:T(1,128)S(1)} %collective-permute-done.28.pool_core, f32[1,1024]{1,0:T(1,128)S(1)} %collective-permute-done.29.pool_chip, ...), custom_call_target="tpu_custom_call" | custom-call | flops 1000000000 | bytes 1048576 | tf_op jit(solution)/shard_map/score/pallas_call | solution.py:367
  (82 shorter events, 16.5 us)
Async XLA Ops:
  0.7 20.0 %collective-permute-start.13 = (bf16[3,1024,256]{2,1,0:T(8,128)(2,1)}, bf16[3,1024,256]{2,1,0:T(8,128)(2,1)S(1)}, u32[]{:S(2)}, u32[]{:S(2)}) collective-permute-start(bf16[3,1024,256]{2,1,0:T(8,128)(2,1)} %bitcast.84), channel_id=1, source_target_pairs={{0,1},{1,0},{2,3},{3,2},{4,5},{5,4},{6,7},{7,6},{8,9},{9,8},{10,11... | collective-permute-start | bytes 4718600 | tf_op jit(solution)/shard_map/ppermute | solution.py:45
  1.2 4.3 %collective-permute-start.7 = (s32[2,16]{1,0:T(2,128)}, s32[2,16]{1,0:T(2,128)S(1)}, u32[]{:S(2)}, u32[]{:S(2)}) collective-permute-start(s32[2,16]{1,0:T(2,128)} %param.33), channel_id=1, source_target_pairs={{0,2},{1,3},{2,0},{3,1},{4,6},{5,7},{6,4},{7,5},{8,10},{9,11},{10,... | collective-permute-start | bytes 392 | tf_op jit(solution)/shard_map/ppermute | solution.py:45
  3.7 16.9 %collective-permute-start.12 = (bf16[2,128,1024]{2,1,0:T(8,128)(2,1)}, bf16[2,128,1024]{2,1,0:T(8,128)(2,1)S(1)}, u32[]{:S(2)}, u32[]{:S(2)}) collective-permute-start(bf16[2,128,1024]{2,1,0:T(8,128)(2,1)} %states.1), channel_id=1, source_target_pairs={{0,1},{1,0},{2,3},{3,2},{4,5},{5,4},{6,7},{7,6},{8,9},{9,8},{10,11... | collective-permute-start | bytes 1572872 | tf_op jit(solution)/shard_map/ppermute | solution.py:45
  5.7 14.9 %collective-permute-start.11 = (bf16[2,128,1024]{2,1,0:T(8,128)(2,1)}, bf16[2,128,1024]{2,1,0:T(8,128)(2,1)S(1)}, u32[]{:S(2)}, u32[]{:S(2)}) collective-permute-start(bf16[2,128,1024]{2,1,0:T(8,128)(2,1)} %states.1), channel_id=1, source_target_pairs={{0,2},{1,3},{2,0},{3,1},{4,6},{5,7},{6,4},{7,5},{8,10},{9,11},{10,... | collective-permute-start | bytes 1572872 | tf_op jit(solution)/shard_map/ppermute | solution.py:45
  7.7 3.5 %collective-permute-start.8 = (s32[1,64]{1,0:T(1,128)S(1)}, s32[1,64]{1,0:T(1,128)S(1)}, u32[]{:S(2)}, u32[]{:S(2)}) collective-permute-start(s32[1,64]{1,0:T(1,128)S(1)} %pad_add_fusion.3), channel_id=1, source_target_pairs={{0,4},{4,0},{8,12},{12,8},{16,20},{20,16},{24,28},{28,24},{1,5},{5... | collective-permute-start | bytes 776 | tf_op jit(solution)/shard_map/ppermute | solution.py:45
  11.3 3.6 %collective-permute-start.9 = (s32[2,64]{1,0:T(2,128)S(1)}, s32[2,64]{1,0:T(2,128)S(1)}, u32[]{:S(2)}, u32[]{:S(2)}) collective-permute-start(s32[2,64]{1,0:T(2,128)S(1)} %pad_add_fusion.2), channel_id=1, source_target_pairs={{0,8},{4,12},{8,0},{12,4},{16,24},{20,28},{24,16},{28,20},{1,9},{5... | collective-permute-start | bytes 1544 | tf_op jit(solution)/shard_map/ppermute | solution.py:45
  15.0 4.5 %collective-permute-start.10 = (s32[4,64]{1,0:T(4,128)S(1)}, s32[4,64]{1,0:T(4,128)S(1)}, u32[]{:S(2)}, u32[]{:S(2)}) collective-permute-start(s32[4,64]{1,0:T(4,128)S(1)} %pad_add_fusion.1), channel_id=1, source_target_pairs={{0,16},{4,20},{8,24},{12,28},{16,0},{20,4},{24,8},{28,12},{1,17},{... | collective-permute-start | bytes 3080 | tf_op jit(solution)/shard_map/ppermute | solution.py:45
  23.4 6.1 %collective-permute-start.20 = (bf16[1024,1024]{1,0:T(8,128)(2,1)S(1)}, bf16[1024,1024]{1,0:T(8,128)(2,1)S(1)}, u32[]{:S(2)}, u32[]{:S(2)}) collective-permute-start(bf16[1024,1024]{1,0:T(8,128)(2,1)S(1)} %copy-done.10), channel_id=1, source_target_pairs={{0,1},{1,0},{2,3},{3,2},{4,5},{5,4},{6,7},{7,6},{8,9},{9,8},{10,11... | collective-permute-start | bytes 6291464 | tf_op jit(solution)/shard_map/ppermute | solution.py:45
  23.7 22.9 %collective-permute-start.26 = (bf16[1024,1024]{1,0:T(8,128)(2,1)}, bf16[1024,1024]{1,0:T(8,128)(2,1)S(1)}, u32[]{:S(2)}, u32[]{:S(2)}) collective-permute-start(bf16[1024,1024]{1,0:T(8,128)(2,1)} %refs_11_.3), channel_id=1, source_target_pairs={{0,1},{1,0},{2,3},{3,2},{4,5},{5,4},{6,7},{7,6},{8,9},{9,8},{10,11... | collective-permute-start | bytes 6291464 | tf_op jit(solution)/shard_map/ppermute | solution.py:45
  24.0 9.7 %collective-permute-start.21 = (bf16[128,1024]{1,0:T(8,128)(2,1)S(1)}, bf16[128,1024]{1,0:T(8,128)(2,1)S(1)}, u32[]{:S(2)}, u32[]{:S(2)}) collective-permute-start(bf16[128,1024]{1,0:T(8,128)(2,1)S(1)} %get-tuple-element.147), channel_id=1, source_target_pairs={{0,2},{1,3},{2,0},{3,1},{4,6},{5,7},{6,4},{7,5},{8,10},{9,11},{10,... | collective-permute-start | bytes 786440 | tf_op jit(solution)/shard_map/ppermute | solution.py:45
  27.9 10.2 %collective-permute-start.19 = (bf16[512,256]{1,0:T(8,128)(2,1)S(1)}, bf16[512,256]{1,0:T(8,128)(2,1)S(1)}, u32[]{:S(2)}, u32[]{:S(2)}) collective-permute-start(bf16[512,256]{1,0:T(8,128)(2,1)S(1)} %get-tuple-element.136.here), channel_id=1, source_target_pairs={{0,2},{1,3},{2,0},{3,1},{4,6},{5,7},{6,4},{7,5},{8,10},{9,11},{10,... | collective-permute-start | bytes 786440 | tf_op jit(solution)/shard_map/ppermute | solution.py:45
  33.6 9.3 %collective-permute-start.22 = (bf16[128,1024]{1,0:T(8,128)(2,1)S(1)}, bf16[128,1024]{1,0:T(8,128)(2,1)S(1)}, u32[]{:S(2)}, u32[]{:S(2)}) collective-permute-start(bf16[128,1024]{1,0:T(8,128)(2,1)S(1)} %collective-permute-done.21.half_0), channel_id=1, source_target_pairs={{0,4},{4,0},{8,12},{12,8},{16,20},{20,16},{24,28},{28,24},{1,5},{5... | collective-permute-start | bytes 786440 | tf_op jit(solution)/shard_map/ppermute | solution.py:45
  38.1 8.5 %collective-permute-start.23 = (bf16[512,256]{1,0:T(8,128)(2,1)S(1)}, bf16[512,256]{1,0:T(8,128)(2,1)S(1)}, u32[]{:S(2)}, u32[]{:S(2)}) collective-permute-start(bf16[512,256]{1,0:T(8,128)(2,1)S(1)} %get-tuple-element.145.context), channel_id=1, source_target_pairs={{0,2},{1,3},{2,0},{3,1},{4,6},{5,7},{6,4},{7,5},{8,10},{9,11},{10,... | collective-permute-start | bytes 786440 | tf_op jit(solution)/shard_map/ppermute | solution.py:45
  42.9 3.8 %collective-permute-start.24 = (bf16[128,1024]{1,0:T(8,128)(2,1)S(1)}, bf16[128,1024]{1,0:T(8,128)(2,1)S(1)}, u32[]{:S(2)}, u32[]{:S(2)}) collective-permute-start(bf16[128,1024]{1,0:T(8,128)(2,1)S(1)} %collective-permute-done.21.half_0), channel_id=1, source_target_pairs={{0,1},{1,0},{2,3},{3,2},{4,5},{5,4},{6,7},{7,6},{8,9},{9,8},{10,11... | collective-permute-start | bytes 786440 | tf_op jit(solution)/shard_map/ppermute | solution.py:45
  43.0 3.7 %collective-permute-start.25 = (bf16[128,1024]{1,0:T(8,128)(2,1)S(1)}, bf16[128,1024]{1,0:T(8,128)(2,1)S(1)}, u32[]{:S(2)}, u32[]{:S(2)}) collective-permute-start(bf16[128,1024]{1,0:T(8,128)(2,1)S(1)} %collective-permute-done.22.half_1), channel_id=1, source_target_pairs={{0,1},{1,0},{2,3},{3,2},{4,5},{5,4},{6,7},{7,6},{8,9},{9,8},{10,11... | collective-permute-start | bytes 786440 | tf_op jit(solution)/shard_map/ppermute | solution.py:45
  44.3 9.3 %collective-permute-start.31 = (bf16[1,4,16,1024]{3,2,0,1:T(8,128)(2,1)S(1)}, bf16[1,4,16,1024]{3,2,0,1:T(8,128)(2,1)S(1)}, u32[]{:S(2)}, u32[]{:S(2)}) collective-permute-start(bf16[1,4,16,1024]{3,2,0,1:T(8,128)(2,1)S(1)} %bitcast.70), channel_id=1, source_target_pairs={{0,16},{4,20},{8,24},{12,28},{16,0},{20,4},{24,8},{28,12},{1,17},{... | collective-permute-start | bytes 393224 | tf_op jit(solution)/shard_map/ppermute | solution.py:45
  50.5 14.4 %collective-permute-start.27 = (bf16[256,1024]{1,0:T(8,128)(2,1)S(1)}, bf16[256,1024]{1,0:T(8,128)(2,1)S(1)}, u32[]{:S(2)}, u32[]{:S(2)}) collective-permute-start(bf16[256,1024]{1,0:T(8,128)(2,1)S(1)} %feed_there.1), channel_id=1, source_target_pairs={{0,2},{1,3},{2,0},{3,1},{4,6},{5,7},{6,4},{7,5},{8,10},{9,11},{10,... | collective-permute-start | bytes 1572872 | tf_op jit(solution)/shard_map/ppermute | solution.py:45
  53.6 7.4 %collective-permute-start.34 = (bf16[2,16,1024]{2,1,0:T(8,128)(2,1)S(1)}, bf16[2,16,1024]{2,1,0:T(8,128)(2,1)S(1)}, u32[]{:S(2)}, u32[]{:S(2)}) collective-permute-start(bf16[2,16,1024]{2,1,0:T(8,128)(2,1)S(1)} %get-tuple-element.191), channel_id=1, source_target_pairs={{0,12},{4,8},{8,4},{12,0},{16,28},{20,24},{24,20},{28,16},{1,13},{... | collective-permute-start | bytes 196616 | tf_op jit(solution)/shard_map/ppermute | solution.py:45
  54.7 6.3 %collective-permute-start.32 = (bf16[2,16,1024]{2,1,0:T(8,128)(2,1)S(1)}, bf16[2,16,1024]{2,1,0:T(8,128)(2,1)S(1)}, u32[]{:S(2)}, u32[]{:S(2)}) collective-permute-start(bf16[2,16,1024]{2,1,0:T(8,128)(2,1)S(1)} %get-tuple-element.193), channel_id=1, source_target_pairs={{0,4},{4,0},{8,12},{12,8},{16,20},{20,16},{24,28},{28,24},{1,5},{5... | collective-permute-start | bytes 196616 | tf_op jit(solution)/shard_map/ppermute | solution.py:45
  55.4 5.5 %collective-permute-start.33 = (bf16[2,16,1024]{2,1,0:T(8,128)(2,1)S(1)}, bf16[2,16,1024]{2,1,0:T(8,128)(2,1)S(1)}, u32[]{:S(2)}, u32[]{:S(2)}) collective-permute-start(bf16[2,16,1024]{2,1,0:T(8,128)(2,1)S(1)} %get-tuple-element.194), channel_id=1, source_target_pairs={{0,8},{4,12},{8,0},{12,4},{16,24},{20,28},{24,16},{28,20},{1,9},{5... | collective-permute-start | bytes 196616 | tf_op jit(solution)/shard_map/ppermute | solution.py:45
  61.3 6.1 %collective-permute-start.35 = (bf16[32,1024]{1,0:T(8,128)(2,1)S(1)}, bf16[32,1024]{1,0:T(8,128)(2,1)S(1)}, u32[]{:S(2)}, u32[]{:S(2)}) collective-permute-start(bf16[32,1024]{1,0:T(8,128)(2,1)S(1)} %get-tuple-element.188), channel_id=1, source_target_pairs={{0,2},{1,3},{2,0},{3,1},{4,6},{5,7},{6,4},{7,5},{8,10},{9,11},{10,... | collective-permute-start | bytes 196616 | tf_op jit(solution)/shard_map/ppermute | solution.py:45
  62.4 5.5 %collective-permute-start.37 = (bf16[32,1024]{1,0:T(8,128)(2,1)S(1)}, bf16[32,1024]{1,0:T(8,128)(2,1)S(1)}, u32[]{:S(2)}, u32[]{:S(2)}) collective-permute-start(bf16[32,1024]{1,0:T(8,128)(2,1)S(1)} %get-tuple-element.189), channel_id=1, source_target_pairs={{0,3},{1,2},{2,1},{3,0},{4,7},{5,6},{6,5},{7,4},{8,11},{9,10},{10,... | collective-permute-start | bytes 196616 | tf_op jit(solution)/shard_map/ppermute | solution.py:45
  62.4 5.5 %collective-permute-start.36 = (bf16[32,1024]{1,0:T(8,128)(2,1)S(1)}, bf16[32,1024]{1,0:T(8,128)(2,1)S(1)}, u32[]{:S(2)}, u32[]{:S(2)}) collective-permute-start(bf16[32,1024]{1,0:T(8,128)(2,1)S(1)} %get-tuple-element.190), channel_id=1, source_target_pairs={{0,1},{1,0},{2,3},{3,2},{4,5},{5,4},{6,7},{7,6},{8,9},{9,8},{10,11... | collective-permute-start | bytes 196616 | tf_op jit(solution)/shard_map/ppermute | solution.py:45
  66.1 3.7 %collective-permute-start.29 = (f32[1,1024]{1,0:T(1,128)S(1)}, f32[1,1024]{1,0:T(1,128)S(1)}, u32[]{:S(2)}, u32[]{:S(2)}) collective-permute-start(f32[1,1024]{1,0:T(1,128)S(1)} %get-tuple-element.155.pool), channel_id=1, source_target_pairs={{0,2},{1,3},{2,0},{3,1},{4,6},{5,7},{6,4},{7,5},{8,10},{9,11},{10,... | collective-permute-start | bytes 12296 | tf_op jit(solution)/shard_map/ppermute | solution.py:45
  (19 other events, 141.6 us)

commit v3 on v2

--- a/solution.py
+++ b/solution.py
@@ -634,7 +634,7 @@
     blocks = (mine, from_core, from_chip, from_diag)
     ids = (held, swap(held, "tp", 1))
     w_up_p = swap(after(w_up, from_diag, w_out_p, *ids), "tp", 1)
-    w_down_p = swap(after(w_down, from_diag, w_out_p, *ids), "tp", 1)
+
     w_x0 = swap(w_half, "tp", 2)
 
     blocks, ids, w_out_p = lax.optimization_barrier((blocks, ids, w_out_p))
@@ -644,6 +644,7 @@
         lengths, after(text, w_up_p), w_qkv_p, b_qkv_p, ids, index_rows.shape[0]
     )
     context_1x = swap(context_1, "tp", 2)
+    w_down_p = swap(after(w_down, w_x0, context_0x, context_1), "tp", 1)
     w_x1 = swap(after(w_x0, context_1), "req", 1)
 
     base, keep, send = project_first(

time: 72.4 us -> 76.1 us (1.051)
  waiting for transfers between devices: 15.5 us -> 20.7 us
  starting transfers between devices: 28.9 us -> 27.8 us
    ppermute x32, waiting for transfers between devices: 15.5 us -> 20.7 us  [swap(): return lax.ppermute(value, axis, [(i, i ^ mask) for i in range(count)])]
    ppermute x32, starting transfers between devices: 28.9 us -> 27.8 us  [swap(): return lax.ppermute(value, axis, [(i, i ^ mask) for i in range(count)])]
  transfers between devices with their start and end apart: 32 -> 32, of which waited for: 12 -> 13; matrix products, arithmetic and copies ran while one was open for 2% -> 2% of each run, Pallas kernels for 32% -> 30%
where the time goes in v3:
time: 76.1 us; the launch traced here: 75.8 us
  starting transfers between devices  27.8 us (37%)
  Pallas kernels  24.4 us (32%)
  waiting for transfers between devices  20.7 us (27%)
  between operations  0.93 us (1%)
  local copies, waits for them, and re-layouts  0.91 us (1%)
    ppermute x32, starting transfers between devices, swap(): return lax.ppermute(value, axis, [(i, i ^ mask) for i in range(count)])  27.8 us
    ppermute x32, waiting for transfers between devices, swap(): return lax.ppermute(value, axis, [(i, i ^ mask) for i in range(count)])  20.7 us
    pallas_call x2, Pallas kernels, feed_forward(): pl.pallas_call(lambda *refs: feed_kernel(keep_rest, *refs), out_shape=jax...  7.62 us
    pallas_call x1, Pallas kernels, second_attention(): pl.pallas_call(functools.partial(second_attention_kernel, rows_here), out...  4.11 us
    pallas_call x1, Pallas kernels, project_first(): pl.pallas_call(project_first_kernel, out_shape=(jax.ShapeDtypeStruct((seq...  3.95 us
    pallas_call x1, Pallas kernels, first_attention(): pl.pallas_call(first_attention_kernel, out_shape=(jax.ShapeDtypeStruct((4...  3.44 us
    pallas_call x1, Pallas kernels, load(): pl.pallas_call(load_kernel, out_shape=(jax.ShapeDtypeStruct(states.shape[...  1.61 us
    pallas_call x1, Pallas kernels, score(): pl.pallas_call(score_kernel, out_shape=(jax.ShapeDtypeStruct((2, rows.sha...  1.59 us
  transfers between devices with their start and end apart: 32, of which 13 were waited for; matrix products, arithmetic and copies ran while one was open for 2% of the time, Pallas kernels for 30%

profile of v3, /device:TPU:0, one launch (start us, length us, event | category | flops | bytes accessed | tf_op | source)
XLA Modules:
  0.0 75.8 jit_solution(4084221515027738076)
XLA Ops:
  1.2 2.6 %collective-permute-start.7 = (s32[2,16]{1,0:T(2,128)}, s32[2,16]{1,0:T(2,128)S(1)}, u32[]{:S(2)}, u32[]{:S(2)}) collective-permute-start(s32[2,16]{1,0:T(2,128)} %param.33), channel_id=1, source_target_pairs={{0,2},{1,3},{2,0},{3,1},{4,6},{5,7},{6,4},{7,5},{8,10},{9,11},{10,... | collective-permute-start | bytes 392 | tf_op jit(solution)/shard_map/ppermute | solution.py:45
  5.7 2.0 %collective-permute-start.11 = (bf16[2,128,1024]{2,1,0:T(8,128)(2,1)}, bf16[2,128,1024]{2,1,0:T(8,128)(2,1)S(1)}, u32[]{:S(2)}, u32[]{:S(2)}) collective-permute-start(bf16[2,128,1024]{2,1,0:T(8,128)(2,1)} %states.1), channel_id=1, source_target_pairs={{0,2},{1,3},{2,0},{3,1},{4,6},{5,7},{6,4},{7,5},{8,10},{9,11},{10,... | collective-permute-start | bytes 1572872 | tf_op jit(solution)/shard_map/ppermute | solution.py:45
  7.7 1.5 %collective-permute-start.8 = (s32[1,64]{1,0:T(1,128)S(1)}, s32[1,64]{1,0:T(1,128)S(1)}, u32[]{:S(2)}, u32[]{:S(2)}) collective-permute-start(s32[1,64]{1,0:T(1,128)S(1)} %pad_add_fusion.3), channel_id=1, source_target_pairs={{0,4},{4,0},{8,12},{12,8},{16,20},{20,16},{24,28},{28,24},{1,5},{5... | collective-permute-start | bytes 776 | tf_op jit(solution)/shard_map/ppermute | solution.py:45
  9.2 2.0 %collective-permute-done.8 = s32[1,64]{1,0:T(1,128)S(1)} collective-permute-done((s32[1,64]{1,0:T(1,128)S(1)}, s32[1,64]{1,0:T(1,128)S(1)}, u32[]{:S(2)}, u32[]{:S(2)}) %collective-permute-start.8) | collective-permute-done | bytes 288 | tf_op jit(solution)/shard_map/ppermute | solution.py:45
  11.3 1.6 %collective-permute-start.9 = (s32[2,64]{1,0:T(2,128)S(1)}, s32[2,64]{1,0:T(2,128)S(1)}, u32[]{:S(2)}, u32[]{:S(2)}) collective-permute-start(s32[2,64]{1,0:T(2,128)S(1)} %pad_add_fusion.2), channel_id=1, source_target_pairs={{0,8},{4,12},{8,0},{12,4},{16,24},{20,28},{24,16},{28,20},{1,9},{5... | collective-permute-start | bytes 1544 | tf_op jit(solution)/shard_map/ppermute | solution.py:45
  12.9 2.0 %collective-permute-done.9 = s32[2,64]{1,0:T(2,128)S(1)} collective-permute-done((s32[2,64]{1,0:T(2,128)S(1)}, s32[2,64]{1,0:T(2,128)S(1)}, u32[]{:S(2)}, u32[]{:S(2)}) %collective-permute-start.9) | collective-permute-done | bytes 544 | tf_op jit(solution)/shard_map/ppermute | solution.py:45
  15.0 2.6 %collective-permute-start.10 = (s32[4,64]{1,0:T(4,128)S(1)}, s32[4,64]{1,0:T(4,128)S(1)}, u32[]{:S(2)}, u32[]{:S(2)}) collective-permute-start(s32[4,64]{1,0:T(4,128)S(1)} %pad_add_fusion.1), channel_id=1, source_target_pairs={{0,16},{4,20},{8,24},{12,28},{16,0},{20,4},{24,8},{28,12},{1,17},{... | collective-permute-start | bytes 3080 | tf_op jit(solution)/shard_map/ppermute | solution.py:45
  17.5 1.6 %load.1 = (bf16[128,1024]{1,0:T(8,128)(2,1)S(1)}, bf16[3,1024,256]{2,1,0:T(8,128)(2,1)S(1)}, bf16[128,1024]{1,0:T(8,128)(2,1)S(1)}) custom-call(bf16[2,128,1024]{2,1,0:T(8,128)(2,1)} %states.1, bf16[3,1024,256]{2,1,0:T(8,128)(2,1)} %bitcast.85, bf16[256,1024]{1,0:T(8,128)(2,1)} %w.1), custom_call_target="tpu_custom_call" | custom-call | flops 1 | bytes 1 | tf_op jit(solution)/shard_map/load/pallas_call | solution.py:80
  21.5 1.8 %collective-permute-done.17.i1 = s32[8,64]{1,0:T(8,128)S(1)} collective-permute-done((s32[8,64]{1,0:T(8,128)S(1)}, s32[8,64]{1,0:T(8,128)S(1)}, u32[]{:S(2)}, u32[]{:S(2)}) %collective-permute-start.17) | collective-permute-done | bytes 2080 | tf_op jit(solution)/shard_map/ppermute | solution.py:45
  24.3 3.4 %attention_own.1 = (bf16[512,256]{1,0:T(8,128)(2,1)S(1)}, bf16[512,1024]{1,0:T(8,128)(2,1)S(1)}) custom-call(s32[2]{0:T(128)} %lengths.7, bf16[128,1024]{1,0:T(8,128)(2,1)S(1)} %get-tuple-element.129.mine, bf16[2,128,1024]{2,1,0:T(8,128)(2,1)S(1)} %collective-permute-done.12.s1, bf16[2,128,1024]{2,1,0:T(8,128)(2,1)S(1)} %collective-permute-done.11.s2, ...), custom_call_target="tpu_custom_call" | custom-call | flops 1 | bytes 1 | tf_op jit(solution)/shard_map/attention_own/pallas_call | solution.py:165
  27.7 1.6 %collective-permute-start.19 = (bf16[512,256]{1,0:T(8,128)(2,1)S(1)}, bf16[512,256]{1,0:T(8,128)(2,1)S(1)}, u32[]{:S(2)}, u32[]{:S(2)}) collective-permute-start(bf16[512,256]{1,0:T(8,128)(2,1)S(1)} %get-tuple-element.136.here), channel_id=1, source_target_pairs={{0,2},{1,3},{2,0},{3,1},{4,6},{5,7},{6,4},{7,5},{8,10},{9,11},{10,... | collective-permute-start | bytes 786440 | tf_op jit(solution)/shard_map/ppermute | solution.py:45
  29.3 4.1 %attention_partner.1 = (bf16[512,256]{1,0:T(8,128)(2,1)S(1)}, s32[2,128]{1,0:T(2,128)S(1)}, bf16[128,128]{1,0:T(8,128)(2,1)S(1)}, s32[1]{0:T(128)}) custom-call(s32[2]{0:T(128)} %lengths.7, bf16[512,1024]{1,0:T(8,128)(2,1)S(1)} %get-tuple-element.138.text, bf16[3,1024,256]{2,1,0:T(8,128)(2,1)S(1)} %collective-permute-done.13.w, ...), custom_call_target="tpu_custom_call" | custom-call | flops 6000000000 | bytes 1048576 | tf_op jit(solution)/shard_map/attention_partner/pallas_call | solution.py:184
  33.4 4.4 %collective-permute-done.19.there = bf16[512,256]{1,0:T(8,128)(2,1)S(1)} collective-permute-done((bf16[512,256]{1,0:T(8,128)(2,1)S(1)}, bf16[512,256]{1,0:T(8,128)(2,1)S(1)}, u32[]{:S(2)}, u32[]{:S(2)}) %collective-permute-start.19) | collective-permute-done | bytes 262176 | tf_op jit(solution)/shard_map/ppermute | solution.py:45
  37.8 1.5 %collective-permute-start.22 = (bf16[128,1024]{1,0:T(8,128)(2,1)S(1)}, bf16[128,1024]{1,0:T(8,128)(2,1)S(1)}, u32[]{:S(2)}, u32[]{:S(2)}) collective-permute-start(bf16[128,1024]{1,0:T(8,128)(2,1)S(1)} %collective-permute-done.21.half_0), channel_id=1, source_target_pairs={{0,4},{4,0},{8,12},{12,8},{16,20},{20,16},{24,28},{28,24},{1,5},{5... | collective-permute-start | bytes 786440 | tf_op jit(solution)/shard_map/ppermute | solution.py:45
  39.8 3.9 %project_first.1 = (f32[512,1024]{1,0:T(8,128)S(1)}, bf16[64,1024]{1,0:T(8,128)(2,1)S(1)}, bf16[64,1024]{1,0:T(8,128)(2,1)S(1)}) custom-call(bf16[512,1024]{1,0:T(8,128)(2,1)S(1)} %get-tuple-element.138.text, bf16[512,256]{1,0:T(8,128)(2,1)S(1)} %get-tuple-element.136.here, bf16[256,1024]{1,0:T(8,128)(2,1)S(1)} %copy-done, f32[1,1024]{1,0:T(1,128)S(1)} %bitcast.69, ...), custom_call_target="tpu_custom_call" | custom-call | flops 1000000000 | bytes 1048576 | tf_op jit(solution)/shard_map/project_first/pallas_call | solution.py:224
  43.9 2.6 %collective-permute-done.22.half_1 = bf16[128,1024]{1,0:T(8,128)(2,1)S(1)} collective-permute-done((bf16[128,1024]{1,0:T(8,128)(2,1)S(1)}, bf16[128,1024]{1,0:T(8,128)(2,1)S(1)}, u32[]{:S(2)}, u32[]{:S(2)}) %collective-permute-start.22) | collective-permute-done | bytes 262176 | tf_op jit(solution)/shard_map/ppermute | solution.py:45
  47.3 2.7 %collective-permute-start.31 = (bf16[1,4,16,1024]{3,2,0,1:T(8,128)(2,1)S(1)}, bf16[1,4,16,1024]{3,2,0,1:T(8,128)(2,1)S(1)}, u32[]{:S(2)}, u32[]{:S(2)}) collective-permute-start(bf16[1,4,16,1024]{3,2,0,1:T(8,128)(2,1)S(1)} %bitcast.70), channel_id=1, source_target_pairs={{0,16},{4,20},{8,24},{12,28},{16,0},{20,4},{24,8},{28,12},{1,17},{... | collective-permute-start | bytes 393224 | tf_op jit(solution)/shard_map/ppermute | solution.py:45
  50.0 3.8 %feed_there.1 = bf16[256,1024]{1,0:T(8,128)(2,1)S(1)} custom-call(f32[512,1024]{1,0:T(8,128)S(1)} %project_second.1.refs_0_, bf16[512,256]{1,0:T(8,128)(2,1)S(1)} %collective-permute-done.23.refs_1_, bf16[128,1024]{1,0:T(8,128)(2,1)S(1)} %collective-permute-done.24.refs_2_, bf16[128,1024]{1,0:T(8,128)(2,1)S(1)} %collective-permute-done.25.refs_3_, ...), custom_call_target="tpu_custom_call" | custom-call | flops 8000000000 | bytes 1048576 | tf_op jit(solution)/shard_map/feed_there/pallas_call | solution.py:295
  54.5 2.6 %collective-permute-done.31 = bf16[1,4,16,1024]{3,2,0,1:T(8,128)(2,1)S(1)} collective-permute-done((bf16[1,4,16,1024]{3,2,0,1:T(8,128)(2,1)S(1)}, bf16[1,4,16,1024]{3,2,0,1:T(8,128)(2,1)S(1)}, u32[]{:S(2)}, u32[]{:S(2)}) %collective-permute-start.31) | collective-permute-done | bytes 131104 | tf_op jit(solution)/shard_map/ppermute | solution.py:45
  57.0 1.7 %collective-permute-start.34 = (bf16[2,16,1024]{2,1,0:T(8,128)(2,1)S(1)}, bf16[2,16,1024]{2,1,0:T(8,128)(2,1)S(1)}, u32[]{:S(2)}, u32[]{:S(2)}) collective-permute-start(bf16[2,16,1024]{2,1,0:T(8,128)(2,1)S(1)} %get-tuple-element.191), channel_id=1, source_target_pairs={{0,12},{4,8},{8,4},{12,0},{16,28},{20,24},{24,20},{28,16},{1,13},{... | collective-permute-start | bytes 196616 | tf_op jit(solution)/shard_map/ppermute | solution.py:45
  60.6 3.8 %feed_here.1.here = f32[256,1024]{1,0:T(8,128)S(1)} custom-call(f32[512,1024]{1,0:T(8,128)S(1)} %project_second.1.refs_0_, bf16[512,256]{1,0:T(8,128)(2,1)S(1)} %collective-permute-done.23.refs_1_, bf16[128,1024]{1,0:T(8,128)(2,1)S(1)} %collective-permute-done.24.refs_2_, bf16[128,1024]{1,0:T(8,128)(2,1)S(1)} %collective-permute-done.25.refs_3_, ...), custom_call_target="tpu_custom_call" | custom-call | flops 8000000000 | bytes 1048576 | tf_op jit(solution)/shard_map/feed_here/pallas_call | solution.py:295
  65.3 1.6 %collective-permute-start.36 = (bf16[32,1024]{1,0:T(8,128)(2,1)S(1)}, bf16[32,1024]{1,0:T(8,128)(2,1)S(1)}, u32[]{:S(2)}, u32[]{:S(2)}) collective-permute-start(bf16[32,1024]{1,0:T(8,128)(2,1)S(1)} %get-tuple-element.190), channel_id=1, source_target_pairs={{0,1},{1,0},{2,3},{3,2},{4,5},{5,4},{6,7},{7,6},{8,9},{9,8},{10,11... | collective-permute-start | bytes 196616 | tf_op jit(solution)/shard_map/ppermute | solution.py:45
  66.9 1.7 %collective-permute-done.27.there = bf16[256,1024]{1,0:T(8,128)(2,1)S(1)} collective-permute-done((bf16[256,1024]{1,0:T(8,128)(2,1)S(1)}, bf16[256,1024]{1,0:T(8,128)(2,1)S(1)}, u32[]{:S(2)}, u32[]{:S(2)}) %collective-permute-start.27) | collective-permute-done | bytes 524320 | tf_op jit(solution)/shard_map/ppermute | solution.py:45
  74.2 1.6 %score.1 = (f32[2,16]{1,0:T(2,128)}, bf16[2,128,1024]{2,1,0:T(8,128)(2,1)}) custom-call(s32[2]{0:T(128)S(1)} %copy-done.2, f32[1,1024]{1,0:T(1,128)S(1)} %get-tuple-element.155.pool, f32[1,1024]{1,0:T(1,128)S(1)} %collective-permute-done.28.pool_core, f32[1,1024]{1,0:T(1,128)S(1)} %collective-permute-done.29.pool_chip, ...), custom_call_target="tpu_custom_call" | custom-call | flops 1000000000 | bytes 1048576 | tf_op jit(solution)/shard_map/score/pallas_call | solution.py:367
  (84 shorter events, 16.1 us)
Async XLA Ops:
  0.7 20.0 %collective-permute-start.13 = (bf16[3,1024,256]{2,1,0:T(8,128)(2,1)}, bf16[3,1024,256]{2,1,0:T(8,128)(2,1)S(1)}, u32[]{:S(2)}, u32[]{:S(2)}) collective-permute-start(bf16[3,1024,256]{2,1,0:T(8,128)(2,1)} %bitcast.84), channel_id=1, source_target_pairs={{0,1},{1,0},{2,3},{3,2},{4,5},{5,4},{6,7},{7,6},{8,9},{9,8},{10,11... | collective-permute-start | bytes 4718600 | tf_op jit(solution)/shard_map/ppermute | solution.py:45
  1.2 4.3 %collective-permute-start.7 = (s32[2,16]{1,0:T(2,128)}, s32[2,16]{1,0:T(2,128)S(1)}, u32[]{:S(2)}, u32[]{:S(2)}) collective-permute-start(s32[2,16]{1,0:T(2,128)} %param.33), channel_id=1, source_target_pairs={{0,2},{1,3},{2,0},{3,1},{4,6},{5,7},{6,4},{7,5},{8,10},{9,11},{10,... | collective-permute-start | bytes 392 | tf_op jit(solution)/shard_map/ppermute | solution.py:45
  3.7 16.9 %collective-permute-start.12 = (bf16[2,128,1024]{2,1,0:T(8,128)(2,1)}, bf16[2,128,1024]{2,1,0:T(8,128)(2,1)S(1)}, u32[]{:S(2)}, u32[]{:S(2)}) collective-permute-start(bf16[2,128,1024]{2,1,0:T(8,128)(2,1)} %states.1), channel_id=1, source_target_pairs={{0,1},{1,0},{2,3},{3,2},{4,5},{5,4},{6,7},{7,6},{8,9},{9,8},{10,11... | collective-permute-start | bytes 1572872 | tf_op jit(solution)/shard_map/ppermute | solution.py:45
  5.7 14.9 %collective-permute-start.11 = (bf16[2,128,1024]{2,1,0:T(8,128)(2,1)}, bf16[2,128,1024]{2,1,0:T(8,128)(2,1)S(1)}, u32[]{:S(2)}, u32[]{:S(2)}) collective-permute-start(bf16[2,128,1024]{2,1,0:T(8,128)(2,1)} %states.1), channel_id=1, source_target_pairs={{0,2},{1,3},{2,0},{3,1},{4,6},{5,7},{6,4},{7,5},{8,10},{9,11},{10,... | collective-permute-start | bytes 1572872 | tf_op jit(solution)/shard_map/ppermute | solution.py:45
  7.7 3.5 %collective-permute-start.8 = (s32[1,64]{1,0:T(1,128)S(1)}, s32[1,64]{1,0:T(1,128)S(1)}, u32[]{:S(2)}, u32[]{:S(2)}) collective-permute-start(s32[1,64]{1,0:T(1,128)S(1)} %pad_add_fusion.3), channel_id=1, source_target_pairs={{0,4},{4,0},{8,12},{12,8},{16,20},{20,16},{24,28},{28,24},{1,5},{5... | collective-permute-start | bytes 776 | tf_op jit(solution)/shard_map/ppermute | solution.py:45
  11.3 3.6 %collective-permute-start.9 = (s32[2,64]{1,0:T(2,128)S(1)}, s32[2,64]{1,0:T(2,128)S(1)}, u32[]{:S(2)}, u32[]{:S(2)}) collective-permute-start(s32[2,64]{1,0:T(2,128)S(1)} %pad_add_fusion.2), channel_id=1, source_target_pairs={{0,8},{4,12},{8,0},{12,4},{16,24},{20,28},{24,16},{28,20},{1,9},{5... | collective-permute-start | bytes 1544 | tf_op jit(solution)/shard_map/ppermute | solution.py:45
  15.0 4.5 %collective-permute-start.10 = (s32[4,64]{1,0:T(4,128)S(1)}, s32[4,64]{1,0:T(4,128)S(1)}, u32[]{:S(2)}, u32[]{:S(2)}) collective-permute-start(s32[4,64]{1,0:T(4,128)S(1)} %pad_add_fusion.1), channel_id=1, source_target_pairs={{0,16},{4,20},{8,24},{12,28},{16,0},{20,4},{24,8},{28,12},{1,17},{... | collective-permute-start | bytes 3080 | tf_op jit(solution)/shard_map/ppermute | solution.py:45
  23.4 5.9 %collective-permute-start.20 = (bf16[1024,1024]{1,0:T(8,128)(2,1)S(1)}, bf16[1024,1024]{1,0:T(8,128)(2,1)S(1)}, u32[]{:S(2)}, u32[]{:S(2)}) collective-permute-start(bf16[1024,1024]{1,0:T(8,128)(2,1)S(1)} %copy-done.10), channel_id=1, source_target_pairs={{0,1},{1,0},{2,3},{3,2},{4,5},{5,4},{6,7},{7,6},{8,9},{9,8},{10,11... | collective-permute-start | bytes 6291464 | tf_op jit(solution)/shard_map/ppermute | solution.py:45
  23.7 9.7 %collective-permute-start.21 = (bf16[128,1024]{1,0:T(8,128)(2,1)S(1)}, bf16[128,1024]{1,0:T(8,128)(2,1)S(1)}, u32[]{:S(2)}, u32[]{:S(2)}) collective-permute-start(bf16[128,1024]{1,0:T(8,128)(2,1)S(1)} %get-tuple-element.147), channel_id=1, source_target_pairs={{0,2},{1,3},{2,0},{3,1},{4,6},{5,7},{6,4},{7,5},{8,10},{9,11},{10,... | collective-permute-start | bytes 786440 | tf_op jit(solution)/shard_map/ppermute | solution.py:45
  27.7 10.0 %collective-permute-start.19 = (bf16[512,256]{1,0:T(8,128)(2,1)S(1)}, bf16[512,256]{1,0:T(8,128)(2,1)S(1)}, u32[]{:S(2)}, u32[]{:S(2)}) collective-permute-start(bf16[512,256]{1,0:T(8,128)(2,1)S(1)} %get-tuple-element.136.here), channel_id=1, source_target_pairs={{0,2},{1,3},{2,0},{3,1},{4,6},{5,7},{6,4},{7,5},{8,10},{9,11},{10,... | collective-permute-start | bytes 786440 | tf_op jit(solution)/shard_map/ppermute | solution.py:45
  37.8 12.2 %collective-permute-start.26 = (bf16[1024,1024]{1,0:T(8,128)(2,1)S(1)}, bf16[1024,1024]{1,0:T(8,128)(2,1)S(1)}, u32[]{:S(2)}, u32[]{:S(2)}) collective-permute-start(bf16[1024,1024]{1,0:T(8,128)(2,1)S(1)} %copy-done.11), channel_id=1, source_target_pairs={{0,1},{1,0},{2,3},{3,2},{4,5},{5,4},{6,7},{7,6},{8,9},{9,8},{10,11... | collective-permute-start | bytes 6291464 | tf_op jit(solution)/shard_map/ppermute | solution.py:45
  37.8 8.7 %collective-permute-start.22 = (bf16[128,1024]{1,0:T(8,128)(2,1)S(1)}, bf16[128,1024]{1,0:T(8,128)(2,1)S(1)}, u32[]{:S(2)}, u32[]{:S(2)}) collective-permute-start(bf16[128,1024]{1,0:T(8,128)(2,1)S(1)} %collective-permute-done.21.half_0), channel_id=1, source_target_pairs={{0,4},{4,0},{8,12},{12,8},{16,20},{20,16},{24,28},{28,24},{1,5},{5... | collective-permute-start | bytes 786440 | tf_op jit(solution)/shard_map/ppermute | solution.py:45
  39.3 10.7 %collective-permute-start.23 = (bf16[512,256]{1,0:T(8,128)(2,1)S(1)}, bf16[512,256]{1,0:T(8,128)(2,1)S(1)}, u32[]{:S(2)}, u32[]{:S(2)}) collective-permute-start(bf16[512,256]{1,0:T(8,128)(2,1)S(1)} %get-tuple-element.145.context), channel_id=1, source_target_pairs={{0,2},{1,3},{2,0},{3,1},{4,6},{5,7},{6,4},{7,5},{8,10},{9,11},{10,... | collective-permute-start | bytes 786440 | tf_op jit(solution)/shard_map/ppermute | solution.py:45
  43.8 6.1 %collective-permute-start.24 = (bf16[128,1024]{1,0:T(8,128)(2,1)S(1)}, bf16[128,1024]{1,0:T(8,128)(2,1)S(1)}, u32[]{:S(2)}, u32[]{:S(2)}) collective-permute-start(bf16[128,1024]{1,0:T(8,128)(2,1)S(1)} %collective-permute-done.21.half_0), channel_id=1, source_target_pairs={{0,1},{1,0},{2,3},{3,2},{4,5},{5,4},{6,7},{7,6},{8,9},{9,8},{10,11... | collective-permute-start | bytes 786440 | tf_op jit(solution)/shard_map/ppermute | solution.py:45
  46.5 3.5 %collective-permute-start.25 = (bf16[128,1024]{1,0:T(8,128)(2,1)S(1)}, bf16[128,1024]{1,0:T(8,128)(2,1)S(1)}, u32[]{:S(2)}, u32[]{:S(2)}) collective-permute-start(bf16[128,1024]{1,0:T(8,128)(2,1)S(1)} %collective-permute-done.22.half_1), channel_id=1, source_target_pairs={{0,1},{1,0},{2,3},{3,2},{4,5},{5,4},{6,7},{7,6},{8,9},{9,8},{10,11... | collective-permute-start | bytes 786440 | tf_op jit(solution)/shard_map/ppermute | solution.py:45
  47.3 9.7 %collective-permute-start.31 = (bf16[1,4,16,1024]{3,2,0,1:T(8,128)(2,1)S(1)}, bf16[1,4,16,1024]{3,2,0,1:T(8,128)(2,1)S(1)}, u32[]{:S(2)}, u32[]{:S(2)}) collective-permute-start(bf16[1,4,16,1024]{3,2,0,1:T(8,128)(2,1)S(1)} %bitcast.70), channel_id=1, source_target_pairs={{0,16},{4,20},{8,24},{12,28},{16,0},{20,4},{24,8},{28,12},{1,17},{... | collective-permute-start | bytes 393224 | tf_op jit(solution)/shard_map/ppermute | solution.py:45
  53.9 14.8 %collective-permute-start.27 = (bf16[256,1024]{1,0:T(8,128)(2,1)S(1)}, bf16[256,1024]{1,0:T(8,128)(2,1)S(1)}, u32[]{:S(2)}, u32[]{:S(2)}) collective-permute-start(bf16[256,1024]{1,0:T(8,128)(2,1)S(1)} %feed_there.1), channel_id=1, source_target_pairs={{0,2},{1,3},{2,0},{3,1},{4,6},{5,7},{6,4},{7,5},{8,10},{9,11},{10,... | collective-permute-start | bytes 1572872 | tf_op jit(solution)/shard_map/ppermute | solution.py:45
  57.0 7.4 %collective-permute-start.34 = (bf16[2,16,1024]{2,1,0:T(8,128)(2,1)S(1)}, bf16[2,16,1024]{2,1,0:T(8,128)(2,1)S(1)}, u32[]{:S(2)}, u32[]{:S(2)}) collective-permute-start(bf16[2,16,1024]{2,1,0:T(8,128)(2,1)S(1)} %get-tuple-element.191), channel_id=1, source_target_pairs={{0,12},{4,8},{8,4},{12,0},{16,28},{20,24},{24,20},{28,16},{1,13},{... | collective-permute-start | bytes 196616 | tf_op jit(solution)/shard_map/ppermute | solution.py:45
  58.8 5.7 %collective-permute-start.32 = (bf16[2,16,1024]{2,1,0:T(8,128)(2,1)S(1)}, bf16[2,16,1024]{2,1,0:T(8,128)(2,1)S(1)}, u32[]{:S(2)}, u32[]{:S(2)}) collective-permute-start(bf16[2,16,1024]{2,1,0:T(8,128)(2,1)S(1)} %get-tuple-element.193), channel_id=1, source_target_pairs={{0,4},{4,0},{8,12},{12,8},{16,20},{20,16},{24,28},{28,24},{1,5},{5... | collective-permute-start | bytes 196616 | tf_op jit(solution)/shard_map/ppermute | solution.py:45
  59.3 5.2 %collective-permute-start.33 = (bf16[2,16,1024]{2,1,0:T(8,128)(2,1)S(1)}, bf16[2,16,1024]{2,1,0:T(8,128)(2,1)S(1)}, u32[]{:S(2)}, u32[]{:S(2)}) collective-permute-start(bf16[2,16,1024]{2,1,0:T(8,128)(2,1)S(1)} %get-tuple-element.194), channel_id=1, source_target_pairs={{0,8},{4,12},{8,0},{12,4},{16,24},{20,28},{24,16},{28,20},{1,9},{5... | collective-permute-start | bytes 196616 | tf_op jit(solution)/shard_map/ppermute | solution.py:45
  64.7 5.7 %collective-permute-start.35 = (bf16[32,1024]{1,0:T(8,128)(2,1)S(1)}, bf16[32,1024]{1,0:T(8,128)(2,1)S(1)}, u32[]{:S(2)}, u32[]{:S(2)}) collective-permute-start(bf16[32,1024]{1,0:T(8,128)(2,1)S(1)} %get-tuple-element.188), channel_id=1, source_target_pairs={{0,2},{1,3},{2,0},{3,1},{4,6},{5,7},{6,4},{7,5},{8,10},{9,11},{10,... | collective-permute-start | bytes 196616 | tf_op jit(solution)/shard_map/ppermute | solution.py:45
  65.3 6.4 %collective-permute-start.37 = (bf16[32,1024]{1,0:T(8,128)(2,1)S(1)}, bf16[32,1024]{1,0:T(8,128)(2,1)S(1)}, u32[]{:S(2)}, u32[]{:S(2)}) collective-permute-start(bf16[32,1024]{1,0:T(8,128)(2,1)S(1)} %get-tuple-element.189), channel_id=1, source_target_pairs={{0,3},{1,2},{2,1},{3,0},{4,7},{5,6},{6,5},{7,4},{8,11},{9,10},{10,... | collective-permute-start | bytes 196616 | tf_op jit(solution)/shard_map/ppermute | solution.py:45
  65.3 6.4 %collective-permute-start.36 = (bf16[32,1024]{1,0:T(8,128)(2,1)S(1)}, bf16[32,1024]{1,0:T(8,128)(2,1)S(1)}, u32[]{:S(2)}, u32[]{:S(2)}) collective-permute-start(bf16[32,1024]{1,0:T(8,128)(2,1)S(1)} %get-tuple-element.190), channel_id=1, source_target_pairs={{0,1},{1,0},{2,3},{3,2},{4,5},{5,4},{6,7},{7,6},{8,9},{9,8},{10,11... | collective-permute-start | bytes 196616 | tf_op jit(solution)/shard_map/ppermute | solution.py:45
  69.8 3.7 %collective-permute-start.29 = (f32[1,1024]{1,0:T(1,128)S(1)}, f32[1,1024]{1,0:T(1,128)S(1)}, u32[]{:S(2)}, u32[]{:S(2)}) collective-permute-start(f32[1,1024]{1,0:T(1,128)S(1)} %get-tuple-element.155.pool), channel_id=1, source_target_pairs={{0,2},{1,3},{2,0},{3,1},{4,6},{5,7},{6,4},{7,5},{8,10},{9,11},{10,... | collective-permute-start | bytes 12296 | tf_op jit(solution)/shard_map/ppermute | solution.py:45
  (20 other events, 159.3 us)
